TPU v7x, 32 devices: a whole 2x2x4 slice. The times are simulated.
32 devices in a mesh: row: 8 (over y, x, core), col: 4 (over z).
Axes of the slice: x: 2, y: 2, z: 4, core: 2. Of those that a mesh axis runs over, the one named last changes fastest.
Arguments:
- density: bfloat16 [1024, 1024], P('row', 'col'), as said below
- cotangent: bfloat16 [1024, 1024], P('row', 'col'), may hold values from -6 to 6
- block_pattern: int32 [16, 16], P('row', 'col'), may hold values from 0 to 1, as said below
- filter_pattern: int32 [16, 16], P('row', 'col'), may hold values from 0 to 1, as said below
Outputs:
- purified: bfloat16 [1024, 1024], P('row', 'col')
- gradient: bfloat16 [1024, 1024], P('row', 'col')
Inputs may be any that keep to these rules, and one draw needn't show every extreme that they name: density is symmetric. `block_pattern`: symmetric, with ones on the diagonal. `filter_pattern`: symmetric, with ones on the diagonal.
All inputs are finite; a program needn't handle non-finite values.
Results may differ from a plain program's by a relative error of at most 0.0043.
Values may be sent and summed in bfloat16 or wider, within the bound.
No kernel may reach another device: no remote copies, remote signals or barrier semaphores. Data moves between devices by JAX's collectives and lax.ppermute only.
A program may use at most 64 MiB of HBM per device.

v0:
```python
import jax
import jax.numpy as jnp
from jax import lax
from jax.experimental import pallas as pl
from jax.experimental.pallas import tpu as pltpu
from jax.sharding import PartitionSpec as P

IN_HBM = pl.BlockSpec(memory_space=pltpu.HBM)
IN_VMEM = pl.BlockSpec(memory_space=pltpu.VMEM)
LIMIT = pltpu.CompilerParams(vmem_limit_bytes=32 * 1024 * 1024)
EARLY = pl.CostEstimate(flops=6_000_000_000, bytes_accessed=0, transcendentals=0)


def dot(a, b):
    return jnp.dot(a, b, preferred_element_type=jnp.float32)


def mask(density, cotangent, block_pattern, filter_pattern):
    height, width = density.shape
    block_size = height // block_pattern.shape[0]

    def kernel(*refs):
        pattern_refs, dense_refs = refs[:2], refs[2:4]
        pair_ref, kept_ref, pattern_held, dense_held, sems = refs[4:]
        copies = []
        for k in range(2):
            copies.append(pltpu.make_async_copy(pattern_refs[k], pattern_held.at[k], sems.at[k]))
            copies.append(pltpu.make_async_copy(dense_refs[k], dense_held.at[k], sems.at[2 + k]))
        for copy in copies:
            copy.start()
        for copy in copies:
            copy.wait()
        lane = lax.broadcasted_iota(jnp.int32, (block_size, width), 1) // block_size
        for k in range(2):
            for i in range(height // block_size):
                rows = pl.ds(i * block_size, block_size)
                kept = jnp.zeros((block_size, width), jnp.float32)
                for j in range(width // block_size):
                    kept = jnp.where(lane == j, pattern_held[k, i, j].astype(jnp.float32), kept)
                kept_ref[k, rows, :] = kept
                pair_ref[k, rows, :] = (dense_held[k, rows, :].astype(jnp.float32) * kept).astype(pair_ref.dtype)

    inputs = (block_pattern, filter_pattern, density, cotangent)
    return pl.pallas_call(
        kernel,
        out_shape=(
            pltpu.VMEM((2, height, width), density.dtype),
            pltpu.VMEM((2, height, width), jnp.float32),
        ),
        in_specs=[IN_HBM] * 4,
        out_specs=(IN_VMEM, IN_VMEM),
        scratch_shapes=[
            pltpu.SMEM((2,) + block_pattern.shape, jnp.int32),
            pltpu.VMEM((2, height, width), density.dtype),
            pltpu.SemaphoreType.DMA((4,)),
        ],
        compiler_params=LIMIT,
        name="mask",
    )(*(pltpu.with_memory_space_constraint(x, pltpu.HBM) for x in inputs))


def settle(block):
    def kernel(block_ref, out_ref):
        out_ref[...] = block_ref[...]

    return pl.pallas_call(
        kernel,
        out_shape=pltpu.VMEM(block.shape, block.dtype),
        in_specs=[IN_VMEM],
        out_specs=IN_VMEM,
        cost_estimate=EARLY,
        compiler_params=LIMIT,
        name="settle",
    )(block)


def flips_of(size):
    flips = []
    while 2 ** len(flips) < size:
        flips.insert(0, 2 ** len(flips))
    return flips


def swap(held, axis_name, size, flips):
    return [
        ([at ^ flip for at in ats], lax.ppermute(blocks, axis_name, [(i, i ^ flip) for i in range(size)]))
        for flip in flips
        for ats, blocks in held
    ]


def double(held, axis_name, size, flips):
    for flip in flips:
        ats = [at for entry in held for at in entry[0]]
        blocks = held[0][1] if len(held) == 1 else jnp.concatenate([entry[1] for entry in held])
        held = held + swap([(ats, blocks)], axis_name, size, [flip])
    return held


def forward(held, axis_name, size, flips):
    held = double(held, axis_name, size, flips[:-2])
    far = swap(held, axis_name, size, flips[-2:-1])
    near = swap(held, axis_name, size, flips[-1:])
    return held + far + near + swap(far, axis_name, size, flips[-1:])


def tie(helds):
    arrays = lax.optimization_barrier([[blocks for _, blocks in held] for held in helds])
    return [[(ats, block) for (ats, _), block in zip(held, blocks)] for held, blocks in zip(helds, arrays)]


def exchange(pair, axis_name, size, settled):
    flips = flips_of(size)
    held = double([([0], pair[None])], axis_name, size, flips[:-2])
    far = swap(held, axis_name, size, flips[-2:-1])
    near = swap(held, axis_name, size, flips[-1:])
    near, far = tie([near, far])
    last = swap(far, axis_name, size, flips[-1:])
    if settled:
        last = [(ats, settle(pairs)) for ats, pairs in last]
    held = held + far + near + last
    return [(at, ((pairs, (k, 0)), (pairs, (k, 1)))) for ats, pairs in held for k, at in enumerate(ats)]


def pieces_of(held, refs):
    for (ats, _), ref in zip(held, refs):
        for k, at in enumerate(ats):
            yield at, ref.at[k]


def part(ref, owner, size):
    return ref.at[pl.ds(pl.multiple_of(owner * size, size), size), :]


def settle(block):
    def kernel(block_ref, out_ref):
        out_ref[...] = block_ref[...]

    return pl.pallas_call(
        kernel,
        out_shape=pltpu.VMEM(block.shape, block.dtype),
        in_specs=[IN_VMEM],
        out_specs=IN_VMEM,
        cost_estimate=EARLY,
        compiler_params=LIMIT,
        name="settle",
    )(block)


def call(kernel, name, fixed, helds, cols, out_shape, scratch=(), hint=None):
    arrays = [*fixed]
    for held in helds:
        arrays += [blocks for _, blocks in held]
    places = {}
    for entry in (entry for held in cols for entry in held):
        for array, _ in entry[1]:
            if id(array) not in places:
                places[id(array)] = len(arrays)
                arrays.append(array)

    def body(*refs):
        fixed_refs, start, lists = refs[:len(fixed)], len(fixed), []
        for held in helds:
            lists.append(refs[start:start + len(held)])
            start += len(held)
        col_refs = [
            [(at, [refs[places[id(array)]].at[k] for array, k in blocks]) for at, blocks in held]
            for held in cols
        ]
        here = (lax.axis_index("row"), lax.axis_index("col"))
        kernel(here, fixed_refs, lists, col_refs, refs[len(arrays):])

    return pl.pallas_call(
        body,
        out_shape=out_shape,
        in_specs=[IN_VMEM] * len(arrays),
        out_specs=jax.tree.map(lambda _: IN_VMEM, out_shape),
        scratch_shapes=scratch,
        cost_estimate=hint,
        compiler_params=LIMIT,
        name=name,
    )(*arrays)


def fill_rows(rows_ref, pieces, here_col):
    height, width = rows_ref.shape[0] // 2, rows_ref.shape[1] // len(pieces)
    for at, blocks in pieces:
        columns = pl.ds(pl.multiple_of((here_col ^ at) * width, width), width)
        for k in range(2):
            rows_ref[k * height:(k + 1) * height, columns] = blocks[k][...]


def square_step(pair, kept, row_held, pair_held):
    _, height, width = pair.shape
    n_row = sum(len(ats) for ats, _ in row_held)

    def kernel(here, fixed, lists, cols, outs):
        pair_ref, kept_ref = fixed
        both_ref, masked_ref, rows_ref = outs
        fill_rows(rows_ref, cols[0], here[1])
        for at, block in pieces_of(row_held, lists[0]):
            part(masked_ref, here[0] ^ at, height)[...] = block[...]
        total = dot(rows_ref[...], masked_ref[...])
        both_ref[0] = (total[:height] * kept_ref[1]).astype(both_ref.dtype)
        grad = 3.0 * pair_ref[1].astype(jnp.float32) - 2.0 * total[height:]
        both_ref[1] = (grad * kept_ref[1]).astype(both_ref.dtype)

    out = (
        pltpu.VMEM((2, height, width), pair.dtype),
        pltpu.VMEM((n_row * height, width), pair.dtype),
        pltpu.VMEM((2 * height, len(pair_held) * width), pair.dtype),
    )
    return call(kernel, "square_step", (pair, kept), (row_held,), (pair_held,), out)


def purify_step(both, kept, masked_cols, both_held):
    _, height, width = both.shape

    def kernel(here, fixed, lists, cols, outs):
        both_ref, kept_ref, masked_ref = fixed
        purified_ref, back_ref, scaled_ref, rows_ref = outs
        fill_rows(rows_ref, cols[0], here[1])
        total = dot(rows_ref[...], masked_ref[...])
        cubic = total[:height] * kept_ref[1]
        purified_ref[...] = (3.0 * both_ref[0].astype(jnp.float32) - 2.0 * cubic).astype(purified_ref.dtype)
        back_ref[...] = total[height:]
        scaled_ref[...] = (-2.0 * rows_ref[:height].astype(jnp.float32)).astype(scaled_ref.dtype)

    rows = (2 * height, len(both_held) * width)
    out = (
        pltpu.VMEM((height, width), both.dtype),
        pltpu.VMEM((height, width), jnp.float32),
        pltpu.VMEM((height, rows[1]), both.dtype),
    )
    scratch = [pltpu.VMEM(rows, both.dtype)]
    return call(kernel, "purify_step", (both, kept, masked_cols), (), (both_held,), out, scratch, hint=EARLY)


def last_step(kept, purified, back, pair_rows, scaled_rows, late_held):
    height, width = back.shape
    n_row = sum(len(ats) for ats, _ in late_held)

    def kernel(here, fixed, lists, cols, outs):
        kept_ref, purified_ref, back_ref, pair_ref, scaled_ref = fixed
        out_ref, gradient_ref, late_cols = outs
        out_ref[...] = purified_ref[...]
        for at, block in pieces_of(late_held, lists[0]):
            for k in range(2):
                part(late_cols.at[k], here[0] ^ at, height)[...] = block[k]
        summed = back_ref[...] + dot(pair_ref[:height], late_cols[0])
        summed = summed + dot(scaled_ref[...], late_cols[1])
        gradient_ref[...] = (summed * kept_ref[0]).astype(gradient_ref.dtype)

    out = jax.ShapeDtypeStruct((height, width), purified.dtype)
    scratch = [pltpu.VMEM((2, n_row * height, width), purified.dtype)]
    fixed = (kept, purified, back, pair_rows, scaled_rows)
    return call(kernel, "last_step", fixed, (late_held,), (), (out, out), scratch)


def on_device(n_row, n_col, density, cotangent, block_pattern, filter_pattern):
    chip_flips, core_flips = flips_of(n_row)[:-1], flips_of(n_row)[-1:]
    pair, kept = mask(density, cotangent, block_pattern, filter_pattern)

    pair_held = exchange(pair, "col", n_col, True)
    row_held = forward([([0], pair[:1])], "row", n_row, chip_flips)
    row_held = double(row_held, "row", n_row, core_flips)
    both, masked_cols, pair_rows = square_step(pair, kept, row_held, pair_held)

    both_held = exchange(both, "col", n_col, False)
    late_held = forward([([0], jnp.stack([both[1], pair[1]])[None])], "row", n_row, chip_flips)
    late_held = double(late_held, "row", n_row, core_flips)
    purified, back, scaled_rows = purify_step(both, kept, masked_cols, both_held)
    return last_step(kept, purified, back, pair_rows, scaled_rows, late_held)


def solution(mesh):
    placed = (P("row", "col"), P("row", "col"), P("row", "col"), P("row", "col"))

    def local(*arrays):
        return on_device(mesh.shape["row"], mesh.shape["col"], *arrays)

    return jax.shard_map(
        local,
        mesh=mesh,
        in_specs=placed,
        out_specs=(P("row", "col"), P("row", "col")),
        check_vma=False,
    )
```

profile of v0, /device:TPU:0, one launch (start us, length us, event | category | flops | bytes accessed | tf_op | source)
XLA Modules:
  0.0 35.3 jit_solution(9619845380102797480)
XLA Ops:
  0.6 0.9 %mask.1 = (bf16[2,128,256]{2,1,0:T(8,128)(2,1)S(1)}, f32[2,128,256]{2,1,0:T(8,128)S(1)}) custom-call(s32[2,4]{1,0:T(2,128)} %refs_0_.1, s32[2,4]{1,0:T(2,128)} %refs_1_.1, bf16[128,256]{1,0:T(8,128)(2,1)} %refs_2_.1, bf16[128,256]{1,0:T(8,128)(2,1)} %refs_3_.1), custom_call_target="tpu_custom_call" | custom-call | tf_op jit(solution)/shard_map/mask/pallas_call | solution.py:44
  1.6 4.1 %collective-permute-start.5 = (bf16[1,2,128,256]{3,2,1,0:T(8,128)(2,1)S(1)}, bf16[1,2,128,256]{3,2,1,0:T(8,128)(2,1)S(1)}, u32[]{:S(2)}, u32[]{:S(2)}) collective-permute-start(bf16[1,2,128,256]{3,2,1,0:T(8,128)(2,1)S(1)} %bitcast.4), channel_id=1, source_target_pairs={{0,2},{1,3},{2,0},{3,1},{4,6},{5,7},{6,4},{7,5},{8,10},{9,11},{10,... | collective-permute-start | bytes 393224 | tf_op jit(solution)/shard_map/ppermute | solution.py:86
  5.7 1.6 %collective-permute-start.4 = (bf16[1,2,128,256]{3,2,1,0:T(8,128)(2,1)S(1)}, bf16[1,2,128,256]{3,2,1,0:T(8,128)(2,1)S(1)}, u32[]{:S(2)}, u32[]{:S(2)}) collective-permute-start(bf16[1,2,128,256]{3,2,1,0:T(8,128)(2,1)S(1)} %bitcast.5), channel_id=1, source_target_pairs={{0,1},{1,0},{2,3},{3,2},{4,5},{5,4},{6,7},{7,6},{8,9},{9,8},{10,11... | collective-permute-start | bytes 393224 | tf_op jit(solution)/shard_map/ppermute | solution.py:86
  7.3 1.6 %collective-permute-start = (bf16[1,128,256]{2,1,0:T(8,128)(2,1)S(1)}, bf16[1,128,256]{2,1,0:T(8,128)(2,1)S(1)}, u32[]{:S(2)}, u32[]{:S(2)}) collective-permute-start(bf16[1,128,256]{2,1,0:T(8,128)(2,1)S(1)} %get-tuple-element.27.refs_2_), channel_id=1, source_target_pairs={{0,16},{4,20},{8,24},{12,28},{16,0},{20,4},{24,8},{28,12},{1,17},{... | collective-permute-start | bytes 196616 | tf_op jit(solution)/shard_map/ppermute | solution.py:86
  8.9 1.5 %collective-permute-start.1 = (bf16[1,128,256]{2,1,0:T(8,128)(2,1)S(1)}, bf16[1,128,256]{2,1,0:T(8,128)(2,1)S(1)}, u32[]{:S(2)}, u32[]{:S(2)}) collective-permute-start(bf16[1,128,256]{2,1,0:T(8,128)(2,1)S(1)} %get-tuple-element.27.refs_2_), channel_id=1, source_target_pairs={{0,8},{4,12},{8,0},{12,4},{16,24},{20,28},{24,16},{28,20},{1,9},{5... | collective-permute-start | bytes 196616 | tf_op jit(solution)/shard_map/ppermute | solution.py:86
  10.3 1.3 %collective-permute-done.refs_3_ = bf16[1,128,256]{2,1,0:T(8,128)(2,1)S(1)} collective-permute-done((bf16[1,128,256]{2,1,0:T(8,128)(2,1)S(1)}, bf16[1,128,256]{2,1,0:T(8,128)(2,1)S(1)}, u32[]{:S(2)}, u32[]{:S(2)}) %collective-permute-start) | collective-permute-done | bytes 65568 | tf_op jit(solution)/shard_map/ppermute | solution.py:86
  11.6 1.5 %collective-permute-start.2 = (bf16[1,128,256]{2,1,0:T(8,128)(2,1)S(1)}, bf16[1,128,256]{2,1,0:T(8,128)(2,1)S(1)}, u32[]{:S(2)}, u32[]{:S(2)}) collective-permute-start(bf16[1,128,256]{2,1,0:T(8,128)(2,1)S(1)} %collective-permute-done.refs_3_), channel_id=1, source_target_pairs={{0,8},{4,12},{8,0},{12,4},{16,24},{20,28},{24,16},{28,20},{1,9},{5... | collective-permute-start | bytes 196616 | tf_op jit(solution)/shard_map/ppermute | solution.py:86
  13.1 0.6 %collective-permute-start.6 = (bf16[1,2,128,256]{3,2,1,0:T(8,128)(2,1)S(1)}, bf16[1,2,128,256]{3,2,1,0:T(8,128)(2,1)S(1)}, u32[]{:S(2)}, u32[]{:S(2)}) collective-permute-start(bf16[1,2,128,256]{3,2,1,0:T(8,128)(2,1)S(1)} %collective-permute-done.5.refs_8_), channel_id=1, source_target_pairs={{0,1},{1,0},{2,3},{3,2},{4,5},{5,4},{6,7},{7,6},{8,9},{9,8},{10,11... | collective-permute-start | bytes 393224 | tf_op jit(solution)/shard_map/ppermute | solution.py:86
  13.7 2.1 %collective-permute-done.2.refs_5_ = bf16[1,128,256]{2,1,0:T(8,128)(2,1)S(1)} collective-permute-done((bf16[1,128,256]{2,1,0:T(8,128)(2,1)S(1)}, bf16[1,128,256]{2,1,0:T(8,128)(2,1)S(1)}, u32[]{:S(2)}, u32[]{:S(2)}) %collective-permute-start.2) | collective-permute-done | bytes 65568 | tf_op jit(solution)/shard_map/ppermute | solution.py:86
  15.9 0.1 collective-permute-start.3
  16.0 2.1 %collective-permute-done.6.block_ref = bf16[1,2,128,256]{3,2,1,0:T(8,128)(2,1)S(1)} collective-permute-done((bf16[1,2,128,256]{3,2,1,0:T(8,128)(2,1)S(1)}, bf16[1,2,128,256]{3,2,1,0:T(8,128)(2,1)S(1)}, u32[]{:S(2)}, u32[]{:S(2)}) %collective-permute-start.6) | collective-permute-done | bytes 131104 | tf_op jit(solution)/shard_map/ppermute | solution.py:86
  18.1 0.4 %square_step.1 = (bf16[2,128,256]{2,1,0:T(8,128)(2,1)S(1)}, bf16[1024,256]{1,0:T(8,128)(2,1)S(1)}, bf16[256,1024]{1,0:T(8,128)(2,1)S(1)}) custom-call(bf16[2,128,256]{2,1,0:T(8,128)(2,1)S(1)} %get-tuple-element.15.refs_0_, f32[2,128,256]{2,1,0:T(8,128)S(1)} %get-tuple-element.14.refs_1_.refs_0_, bf16[1,128,256]{2,1,0:T(8,128)(2,1)S(1)} %get-tuple-element.27.refs_2_, ...), custom_call_target="tpu_custom_call" | custom-call | tf_op jit(solution)/shard_map/square_step/pallas_call | solution.py:173
  18.5 1.6 %collective-permute-start.10 = (bf16[1,2,128,256]{3,2,1,0:T(8,128)(2,1)S(1)}, bf16[1,2,128,256]{3,2,1,0:T(8,128)(2,1)S(1)}, u32[]{:S(2)}, u32[]{:S(2)}) collective-permute-start(bf16[1,2,128,256]{3,2,1,0:T(8,128)(2,1)S(1)} %maximum_bitcast_fusion.refs_5_), channel_id=1, source_target_pairs={{0,16},{4,20},{8,24},{12,28},{16,0},{20,4},{24,8},{28,12},{1,17},{... | collective-permute-start | bytes 393224 | tf_op jit(solution)/shard_map/ppermute | solution.py:86
  20.1 1.7 %collective-permute-start.8 = (bf16[1,2,128,256]{3,2,1,0:T(8,128)(2,1)S(1)}, bf16[1,2,128,256]{3,2,1,0:T(8,128)(2,1)S(1)}, u32[]{:S(2)}, u32[]{:S(2)}) collective-permute-start(bf16[1,2,128,256]{3,2,1,0:T(8,128)(2,1)S(1)} %bitcast.7), channel_id=1, source_target_pairs={{0,2},{1,3},{2,0},{3,1},{4,6},{5,7},{6,4},{7,5},{8,10},{9,11},{10,... | collective-permute-start | bytes 393224 | tf_op jit(solution)/shard_map/ppermute | solution.py:86
  21.8 1.7 %collective-permute-start.7 = (bf16[1,2,128,256]{3,2,1,0:T(8,128)(2,1)S(1)}, bf16[1,2,128,256]{3,2,1,0:T(8,128)(2,1)S(1)}, u32[]{:S(2)}, u32[]{:S(2)}) collective-permute-start(bf16[1,2,128,256]{3,2,1,0:T(8,128)(2,1)S(1)} %bitcast.8), channel_id=1, source_target_pairs={{0,1},{1,0},{2,3},{3,2},{4,5},{5,4},{6,7},{7,6},{8,9},{9,8},{10,11... | collective-permute-start | bytes 393224 | tf_op jit(solution)/shard_map/ppermute | solution.py:86
  23.6 1.5 %collective-permute-start.11 = (bf16[1,2,128,256]{3,2,1,0:T(8,128)(2,1)S(1)}, bf16[1,2,128,256]{3,2,1,0:T(8,128)(2,1)S(1)}, u32[]{:S(2)}, u32[]{:S(2)}) collective-permute-start(bf16[1,2,128,256]{3,2,1,0:T(8,128)(2,1)S(1)} %maximum_bitcast_fusion.refs_5_), channel_id=1, source_target_pairs={{0,8},{4,12},{8,0},{12,4},{16,24},{20,28},{24,16},{28,20},{1,9},{5... | collective-permute-start | bytes 393224 | tf_op jit(solution)/shard_map/ppermute | solution.py:86
  25.1 0.5 %collective-permute-start.12 = (bf16[1,2,128,256]{3,2,1,0:T(8,128)(2,1)S(1)}, bf16[1,2,128,256]{3,2,1,0:T(8,128)(2,1)S(1)}, u32[]{:S(2)}, u32[]{:S(2)}) collective-permute-start(bf16[1,2,128,256]{3,2,1,0:T(8,128)(2,1)S(1)} %collective-permute-done.10.refs_6_), channel_id=1, source_target_pairs={{0,8},{4,12},{8,0},{12,4},{16,24},{20,28},{24,16},{28,20},{1,9},{5... | collective-permute-start | bytes 393224 | tf_op jit(solution)/shard_map/ppermute | solution.py:86
  25.6 2.9 %collective-permute-done.8.refs_4_ = bf16[1,2,128,256]{3,2,1,0:T(8,128)(2,1)S(1)} collective-permute-done((bf16[1,2,128,256]{3,2,1,0:T(8,128)(2,1)S(1)}, bf16[1,2,128,256]{3,2,1,0:T(8,128)(2,1)S(1)}, u32[]{:S(2)}, u32[]{:S(2)}) %collective-permute-start.8) | collective-permute-done | bytes 131104 | tf_op jit(solution)/shard_map/ppermute | solution.py:86
  28.5 0.4 %collective-permute-done.7.refs_5_ = bf16[1,2,128,256]{3,2,1,0:T(8,128)(2,1)S(1)} collective-permute-done((bf16[1,2,128,256]{3,2,1,0:T(8,128)(2,1)S(1)}, bf16[1,2,128,256]{3,2,1,0:T(8,128)(2,1)S(1)}, u32[]{:S(2)}, u32[]{:S(2)}) %collective-permute-start.7) | collective-permute-done | bytes 131104 | tf_op jit(solution)/shard_map/ppermute | solution.py:86
  28.9 0.4 %collective-permute-start.9 = (bf16[1,2,128,256]{3,2,1,0:T(8,128)(2,1)S(1)}, bf16[1,2,128,256]{3,2,1,0:T(8,128)(2,1)S(1)}, u32[]{:S(2)}, u32[]{:S(2)}) collective-permute-start(bf16[1,2,128,256]{3,2,1,0:T(8,128)(2,1)S(1)} %collective-permute-done.8.refs_4_), channel_id=1, source_target_pairs={{0,1},{1,0},{2,3},{3,2},{4,5},{5,4},{6,7},{7,6},{8,9},{9,8},{10,11... | collective-permute-start | bytes 393224 | tf_op jit(solution)/shard_map/ppermute | solution.py:86
  29.3 0.8 %collective-permute-done.12.refs_8_ = bf16[1,2,128,256]{3,2,1,0:T(8,128)(2,1)S(1)} collective-permute-done((bf16[1,2,128,256]{3,2,1,0:T(8,128)(2,1)S(1)}, bf16[1,2,128,256]{3,2,1,0:T(8,128)(2,1)S(1)}, u32[]{:S(2)}, u32[]{:S(2)}) %collective-permute-start.12) | collective-permute-done | bytes 131104 | tf_op jit(solution)/shard_map/ppermute | solution.py:86
  30.3 3.6 %collective-permute-done.9.refs_6_ = bf16[1,2,128,256]{3,2,1,0:T(8,128)(2,1)S(1)} collective-permute-done((bf16[1,2,128,256]{3,2,1,0:T(8,128)(2,1)S(1)}, bf16[1,2,128,256]{3,2,1,0:T(8,128)(2,1)S(1)}, u32[]{:S(2)}, u32[]{:S(2)}) %collective-permute-start.9) | collective-permute-done | bytes 131104 | tf_op jit(solution)/shard_map/ppermute | solution.py:86
  33.9 0.4 %purify_step.1 = (bf16[128,256]{1,0:T(8,128)(2,1)S(1)}, f32[128,256]{1,0:T(8,128)S(1)}, bf16[128,1024]{1,0:T(8,128)(2,1)S(1)}) custom-call(bf16[2,128,256]{2,1,0:T(8,128)(2,1)S(1)} %get-tuple-element.18.refs_0_, f32[2,128,256]{2,1,0:T(8,128)S(1)} %get-tuple-element.14.refs_1_.refs_0_, bf16[1024,256]{1,0:T(8,128)(2,1)S(1)} %get-tuple-element.19.refs_2_, ...), custom_call_target="tpu_custom_call" | custom-call | flops 6000000000 | tf_op jit(solution)/shard_map/purify_step/pallas_call | solution.py:173
  34.3 1.0 %last_step.1 = (bf16[128,256]{1,0:T(8,128)(2,1)}, bf16[128,256]{1,0:T(8,128)(2,1)}) custom-call(f32[2,128,256]{2,1,0:T(8,128)S(1)} %get-tuple-element.14.refs_1_.refs_0_, bf16[128,256]{1,0:T(8,128)(2,1)S(1)} %get-tuple-element.22.refs_1_, f32[128,256]{1,0:T(8,128)S(1)} %get-tuple-element.23.refs_2_, bf16[256,1024]{1,0:T(8,128)(2,1)S(1)} %get-tuple-element.24.refs_3_, ...), custom_call_target="tpu_custom_call" | custom-call | tf_op jit(solution)/shard_map/last_step/pallas_call | solution.py:173
  (14 shorter events, 0.2 us)
Async XLA Ops:
  1.6 11.5 %collective-permute-start.5 = (bf16[1,2,128,256]{3,2,1,0:T(8,128)(2,1)S(1)}, bf16[1,2,128,256]{3,2,1,0:T(8,128)(2,1)S(1)}, u32[]{:S(2)}, u32[]{:S(2)}) collective-permute-start(bf16[1,2,128,256]{3,2,1,0:T(8,128)(2,1)S(1)} %bitcast.4), channel_id=1, source_target_pairs={{0,2},{1,3},{2,0},{3,1},{4,6},{5,7},{6,4},{7,5},{8,10},{9,11},{10,... | collective-permute-start | bytes 393224 | tf_op jit(solution)/shard_map/ppermute | solution.py:86
  5.7 7.4 %collective-permute-start.4 = (bf16[1,2,128,256]{3,2,1,0:T(8,128)(2,1)S(1)}, bf16[1,2,128,256]{3,2,1,0:T(8,128)(2,1)S(1)}, u32[]{:S(2)}, u32[]{:S(2)}) collective-permute-start(bf16[1,2,128,256]{3,2,1,0:T(8,128)(2,1)S(1)} %bitcast.5), channel_id=1, source_target_pairs={{0,1},{1,0},{2,3},{3,2},{4,5},{5,4},{6,7},{7,6},{8,9},{9,8},{10,11... | collective-permute-start | bytes 393224 | tf_op jit(solution)/shard_map/ppermute | solution.py:86
  7.3 4.3 %collective-permute-start = (bf16[1,128,256]{2,1,0:T(8,128)(2,1)S(1)}, bf16[1,128,256]{2,1,0:T(8,128)(2,1)S(1)}, u32[]{:S(2)}, u32[]{:S(2)}) collective-permute-start(bf16[1,128,256]{2,1,0:T(8,128)(2,1)S(1)} %get-tuple-element.27.refs_2_), channel_id=1, source_target_pairs={{0,16},{4,20},{8,24},{12,28},{16,0},{20,4},{24,8},{28,12},{1,17},{... | collective-permute-start | bytes 196616 | tf_op jit(solution)/shard_map/ppermute | solution.py:86
  8.9 4.9 %collective-permute-start.1 = (bf16[1,128,256]{2,1,0:T(8,128)(2,1)S(1)}, bf16[1,128,256]{2,1,0:T(8,128)(2,1)S(1)}, u32[]{:S(2)}, u32[]{:S(2)}) collective-permute-start(bf16[1,128,256]{2,1,0:T(8,128)(2,1)S(1)} %get-tuple-element.27.refs_2_), channel_id=1, source_target_pairs={{0,8},{4,12},{8,0},{12,4},{16,24},{20,28},{24,16},{28,20},{1,9},{5... | collective-permute-start | bytes 196616 | tf_op jit(solution)/shard_map/ppermute | solution.py:86
  11.6 4.3 %collective-permute-start.2 = (bf16[1,128,256]{2,1,0:T(8,128)(2,1)S(1)}, bf16[1,128,256]{2,1,0:T(8,128)(2,1)S(1)}, u32[]{:S(2)}, u32[]{:S(2)}) collective-permute-start(bf16[1,128,256]{2,1,0:T(8,128)(2,1)S(1)} %collective-permute-done.refs_3_), channel_id=1, source_target_pairs={{0,8},{4,12},{8,0},{12,4},{16,24},{20,28},{24,16},{28,20},{1,9},{5... | collective-permute-start | bytes 196616 | tf_op jit(solution)/shard_map/ppermute | solution.py:86
  13.1 5.0 %collective-permute-start.6 = (bf16[1,2,128,256]{3,2,1,0:T(8,128)(2,1)S(1)}, bf16[1,2,128,256]{3,2,1,0:T(8,128)(2,1)S(1)}, u32[]{:S(2)}, u32[]{:S(2)}) collective-permute-start(bf16[1,2,128,256]{3,2,1,0:T(8,128)(2,1)S(1)} %collective-permute-done.5.refs_8_), channel_id=1, source_target_pairs={{0,1},{1,0},{2,3},{3,2},{4,5},{5,4},{6,7},{7,6},{8,9},{9,8},{10,11... | collective-permute-start | bytes 393224 | tf_op jit(solution)/shard_map/ppermute | solution.py:86
  15.9 2.2 %collective-permute-start.3 = (bf16[4,128,256]{2,1,0:T(8,128)(2,1)S(1)}, bf16[4,128,256]{2,1,0:T(8,128)(2,1)S(1)}, u32[]{:S(2)}, u32[]{:S(2)}) collective-permute-start(bf16[4,128,256]{2,1,0:T(8,128)(2,1)S(1)} %pad_maximum_fusion.1), channel_id=1, source_target_pairs={{0,4},{4,0},{8,12},{12,8},{16,20},{20,16},{24,28},{28,24},{1,5},{5... | collective-permute-start | bytes 786440 | tf_op jit(solution)/shard_map/ppermute | solution.py:86
  18.5 6.5 %collective-permute-start.10 = (bf16[1,2,128,256]{3,2,1,0:T(8,128)(2,1)S(1)}, bf16[1,2,128,256]{3,2,1,0:T(8,128)(2,1)S(1)}, u32[]{:S(2)}, u32[]{:S(2)}) collective-permute-start(bf16[1,2,128,256]{3,2,1,0:T(8,128)(2,1)S(1)} %maximum_bitcast_fusion.refs_5_), channel_id=1, source_target_pairs={{0,16},{4,20},{8,24},{12,28},{16,0},{20,4},{24,8},{28,12},{1,17},{... | collective-permute-start | bytes 393224 | tf_op jit(solution)/shard_map/ppermute | solution.py:86
  20.1 8.4 %collective-permute-start.8 = (bf16[1,2,128,256]{3,2,1,0:T(8,128)(2,1)S(1)}, bf16[1,2,128,256]{3,2,1,0:T(8,128)(2,1)S(1)}, u32[]{:S(2)}, u32[]{:S(2)}) collective-permute-start(bf16[1,2,128,256]{3,2,1,0:T(8,128)(2,1)S(1)} %bitcast.7), channel_id=1, source_target_pairs={{0,2},{1,3},{2,0},{3,1},{4,6},{5,7},{6,4},{7,5},{8,10},{9,11},{10,... | collective-permute-start | bytes 393224 | tf_op jit(solution)/shard_map/ppermute | solution.py:86
  21.8 7.1 %collective-permute-start.7 = (bf16[1,2,128,256]{3,2,1,0:T(8,128)(2,1)S(1)}, bf16[1,2,128,256]{3,2,1,0:T(8,128)(2,1)S(1)}, u32[]{:S(2)}, u32[]{:S(2)}) collective-permute-start(bf16[1,2,128,256]{3,2,1,0:T(8,128)(2,1)S(1)} %bitcast.8), channel_id=1, source_target_pairs={{0,1},{1,0},{2,3},{3,2},{4,5},{5,4},{6,7},{7,6},{8,9},{9,8},{10,11... | collective-permute-start | bytes 393224 | tf_op jit(solution)/shard_map/ppermute | solution.py:86
  23.6 5.7 %collective-permute-start.11 = (bf16[1,2,128,256]{3,2,1,0:T(8,128)(2,1)S(1)}, bf16[1,2,128,256]{3,2,1,0:T(8,128)(2,1)S(1)}, u32[]{:S(2)}, u32[]{:S(2)}) collective-permute-start(bf16[1,2,128,256]{3,2,1,0:T(8,128)(2,1)S(1)} %maximum_bitcast_fusion.refs_5_), channel_id=1, source_target_pairs={{0,8},{4,12},{8,0},{12,4},{16,24},{20,28},{24,16},{28,20},{1,9},{5... | collective-permute-start | bytes 393224 | tf_op jit(solution)/shard_map/ppermute | solution.py:86
  25.1 5.0 %collective-permute-start.12 = (bf16[1,2,128,256]{3,2,1,0:T(8,128)(2,1)S(1)}, bf16[1,2,128,256]{3,2,1,0:T(8,128)(2,1)S(1)}, u32[]{:S(2)}, u32[]{:S(2)}) collective-permute-start(bf16[1,2,128,256]{3,2,1,0:T(8,128)(2,1)S(1)} %collective-permute-done.10.refs_6_), channel_id=1, source_target_pairs={{0,8},{4,12},{8,0},{12,4},{16,24},{20,28},{24,16},{28,20},{1,9},{5... | collective-permute-start | bytes 393224 | tf_op jit(solution)/shard_map/ppermute | solution.py:86
  28.9 5.0 %collective-permute-start.9 = (bf16[1,2,128,256]{3,2,1,0:T(8,128)(2,1)S(1)}, bf16[1,2,128,256]{3,2,1,0:T(8,128)(2,1)S(1)}, u32[]{:S(2)}, u32[]{:S(2)}) collective-permute-start(bf16[1,2,128,256]{3,2,1,0:T(8,128)(2,1)S(1)} %collective-permute-done.8.refs_4_), channel_id=1, source_target_pairs={{0,1},{1,0},{2,3},{3,2},{4,5},{5,4},{6,7},{7,6},{8,9},{9,8},{10,11... | collective-permute-start | bytes 393224 | tf_op jit(solution)/shard_map/ppermute | solution.py:86
  30.2 4.1 %collective-permute-start.13 = (bf16[4,2,128,256]{3,2,1,0:T(8,128)(2,1)S(1)}, bf16[4,2,128,256]{3,2,1,0:T(8,128)(2,1)S(1)}, u32[]{:S(2)}, u32[]{:S(2)}) collective-permute-start(bf16[4,2,128,256]{3,2,1,0:T(8,128)(2,1)S(1)} %pad_maximum_fusion), channel_id=1, source_target_pairs={{0,4},{4,0},{8,12},{12,8},{16,20},{20,16},{24,28},{28,24},{1,5},{5... | collective-permute-start | bytes 1572872 | tf_op jit(solution)/shard_map/ppermute | solution.py:86
where the time goes:
time: 35.5 us; the launch traced here: 35.3 us
  starting transfers between devices  18.4 us (52%)
  waiting for transfers between devices  13.3 us (37%)
  Pallas kernels  2.74 us (8%)
  between operations  0.73 us (2%)
    ppermute x14, starting transfers between devices, swap(): lax.ppermute(blocks, axis_name, [(i, i ^ flip) for i in range(size)])  18.4 us
    ppermute x14, waiting for transfers between devices, swap(): lax.ppermute(blocks, axis_name, [(i, i ^ flip) for i in range(size)])  13.3 us
    pallas_call x3, Pallas kernels, call(): pl.pallas_call(body, out_shape=out_shape, in_specs=[IN_VMEM] * len(arrays...  1.79 us
    pallas_call x1, Pallas kernels, mask(): pl.pallas_call(kernel, out_shape=(pltpu.VMEM((2, height, width), density....  0.94 us
  transfers between devices with their start and end apart: 14, of which 7 were waited for; matrix products, arithmetic and copies ran while one was open for 0% of the time, Pallas kernels for 1%

commit v1 on v0

--- a/solution.py
+++ b/solution.py
@@ -122,12 +122,6 @@
     return [(at, ((pairs, (k, 0)), (pairs, (k, 1)))) for ats, pairs in held for k, at in enumerate(ats)]
 
 
-def pieces_of(held, refs):
-    for (ats, _), ref in zip(held, refs):
-        for k, at in enumerate(ats):
-            yield at, ref.at[k]
-
-
 def part(ref, owner, size):
     return ref.at[pl.ds(pl.multiple_of(owner * size, size), size), :]
 
@@ -147,28 +141,21 @@
     )(block)
 
 
-def call(kernel, name, fixed, helds, cols, out_shape, scratch=(), hint=None):
-    arrays = [*fixed]
-    for held in helds:
-        arrays += [blocks for _, blocks in held]
-    places = {}
-    for entry in (entry for held in cols for entry in held):
-        for array, _ in entry[1]:
-            if id(array) not in places:
-                places[id(array)] = len(arrays)
-                arrays.append(array)
+def call(kernel, name, fixed, blocks, pairs, out_shape, scratch=(), hint=None):
+    arrays, places = [*fixed], {}
+    for array, _ in [block for _, block in blocks] + [block for _, two in pairs for block in two]:
+        if id(array) not in places:
+            places[id(array)] = len(arrays)
+            arrays.append(array)
 
     def body(*refs):
-        fixed_refs, start, lists = refs[:len(fixed)], len(fixed), []
-        for held in helds:
-            lists.append(refs[start:start + len(held)])
-            start += len(held)
-        col_refs = [
-            [(at, [refs[places[id(array)]].at[k] for array, k in blocks]) for at, blocks in held]
-            for held in cols
-        ]
+        def ref_of(block):
+            return refs[places[id(block[0])]].at[block[1]]
+
         here = (lax.axis_index("row"), lax.axis_index("col"))
-        kernel(here, fixed_refs, lists, col_refs, refs[len(arrays):])
+        block_refs = [(at, ref_of(block)) for at, block in blocks]
+        pair_refs = [(at, [ref_of(block) for block in two]) for at, two in pairs]
+        kernel(here, refs[:len(fixed)], block_refs, pair_refs, refs[len(arrays):])
 
     return pl.pallas_call(
         body,
@@ -190,15 +177,15 @@
             rows_ref[k * height:(k + 1) * height, columns] = blocks[k][...]
 
 
-def square_step(pair, kept, row_held, pair_held):
+def square_step(pair, kept, masked_blocks, pair_held):
     _, height, width = pair.shape
-    n_row = sum(len(ats) for ats, _ in row_held)
-
-    def kernel(here, fixed, lists, cols, outs):
+    n_row = len(masked_blocks)
+
+    def kernel(here, fixed, blocks, pairs, outs):
         pair_ref, kept_ref = fixed
         both_ref, masked_ref, rows_ref = outs
-        fill_rows(rows_ref, cols[0], here[1])
-        for at, block in pieces_of(row_held, lists[0]):
+        fill_rows(rows_ref, pairs, here[1])
+        for at, block in blocks:
             part(masked_ref, here[0] ^ at, height)[...] = block[...]
         total = dot(rows_ref[...], masked_ref[...])
         both_ref[0] = (total[:height] * kept_ref[1]).astype(both_ref.dtype)
@@ -210,16 +197,16 @@
         pltpu.VMEM((n_row * height, width), pair.dtype),
         pltpu.VMEM((2 * height, len(pair_held) * width), pair.dtype),
     )
-    return call(kernel, "square_step", (pair, kept), (row_held,), (pair_held,), out)
+    return call(kernel, "square_step", (pair, kept), masked_blocks, pair_held, out)
 
 
 def purify_step(both, kept, masked_cols, both_held):
     _, height, width = both.shape
 
-    def kernel(here, fixed, lists, cols, outs):
+    def kernel(here, fixed, blocks, pairs, outs):
         both_ref, kept_ref, masked_ref = fixed
         purified_ref, back_ref, scaled_ref, rows_ref = outs
-        fill_rows(rows_ref, cols[0], here[1])
+        fill_rows(rows_ref, pairs, here[1])
         total = dot(rows_ref[...], masked_ref[...])
         cubic = total[:height] * kept_ref[1]
         purified_ref[...] = (3.0 * both_ref[0].astype(jnp.float32) - 2.0 * cubic).astype(purified_ref.dtype)
@@ -233,20 +220,19 @@
         pltpu.VMEM((height, rows[1]), both.dtype),
     )
     scratch = [pltpu.VMEM(rows, both.dtype)]
-    return call(kernel, "purify_step", (both, kept, masked_cols), (), (both_held,), out, scratch, hint=EARLY)
-
-
-def last_step(kept, purified, back, pair_rows, scaled_rows, late_held):
+    return call(kernel, "purify_step", (both, kept, masked_cols), [], both_held, out, scratch, hint=EARLY)
+
+
+def last_step(kept, purified, back, pair_rows, scaled_rows, grad_blocks, filtered_blocks):
     height, width = back.shape
-    n_row = sum(len(ats) for ats, _ in late_held)
-
-    def kernel(here, fixed, lists, cols, outs):
+    n_row = len(grad_blocks)
+
+    def kernel(here, fixed, blocks, pairs, outs):
         kept_ref, purified_ref, back_ref, pair_ref, scaled_ref = fixed
         out_ref, gradient_ref, late_cols = outs
         out_ref[...] = purified_ref[...]
-        for at, block in pieces_of(late_held, lists[0]):
-            for k in range(2):
-                part(late_cols.at[k], here[0] ^ at, height)[...] = block[k]
+        for i, (at, block) in enumerate(blocks):
+            part(late_cols.at[i // n_row], here[0] ^ at, height)[...] = block[...]
         summed = back_ref[...] + dot(pair_ref[:height], late_cols[0])
         summed = summed + dot(scaled_ref[...], late_cols[1])
         gradient_ref[...] = (summed * kept_ref[0]).astype(gradient_ref.dtype)
@@ -254,23 +240,57 @@
     out = jax.ShapeDtypeStruct((height, width), purified.dtype)
     scratch = [pltpu.VMEM((2, n_row * height, width), purified.dtype)]
     fixed = (kept, purified, back, pair_rows, scaled_rows)
-    return call(kernel, "last_step", fixed, (late_held,), (), (out, out), scratch)
+    return call(kernel, "last_step", fixed, grad_blocks + filtered_blocks, [], (out, out), scratch)
+
+
+def take(held, *inner):
+    return [(at, (array, (k,) + inner)) for ats, array in held for k, at in enumerate(ats)]
+
+
+def cut(held, k):
+    return [(ats, array[:, k]) for ats, array in held]
+
+
+def pairs_of(one, two):
+    return [(ats, jnp.stack([first, second], 1)) for (ats, first), (_, second) in zip(one, two)]
+
+
+def across_cores(lists, n_row):
+    ats = [[at for ats, _ in held for at in ats] for held in lists]
+    assert all(sorted(a) == sorted(ats[0]) for a in ats)
+    flips = flips_of(n_row)[-1:]
+    sent = jnp.stack([jnp.concatenate([array for _, array in held]) for held in lists])
+    got = [lax.ppermute(sent, "row", [(i, i ^ flip) for i in range(n_row)]) for flip in flips]
+    return [
+        take(held) + [(at ^ flip, (array, (k, i))) for flip, array in zip(flips, got) for i, at in enumerate(own)]
+        for k, (held, own) in enumerate(zip(lists, ats))
+    ]
 
 
 def on_device(n_row, n_col, density, cotangent, block_pattern, filter_pattern):
-    chip_flips, core_flips = flips_of(n_row)[:-1], flips_of(n_row)[-1:]
+    chip_flips = flips_of(n_row)[:-1]
+    lead, first, second = chip_flips[:-2], chip_flips[-2:-1], chip_flips[-1:]
     pair, kept = mask(density, cotangent, block_pattern, filter_pattern)
 
     pair_held = exchange(pair, "col", n_col, True)
-    row_held = forward([([0], pair[:1])], "row", n_row, chip_flips)
-    row_held = double(row_held, "row", n_row, core_flips)
-    both, masked_cols, pair_rows = square_step(pair, kept, row_held, pair_held)
+    own = double([([0], pair[None])], "row", n_row, lead)
+    masked = cut(own, 0)
+    far = swap(masked, "row", n_row, first)
+    near = swap(own, "row", n_row, second)
+    masked = masked + far + cut(near, 0) + swap(far, "row", n_row, second)
+    (masked_blocks,) = across_cores([masked], n_row)
+    both, masked_cols, pair_rows = square_step(pair, kept, masked_blocks, pair_held)
 
     both_held = exchange(both, "col", n_col, False)
-    late_held = forward([([0], jnp.stack([both[1], pair[1]])[None])], "row", n_row, chip_flips)
-    late_held = double(late_held, "row", n_row, core_flips)
+    grad = double([([0], both[1:])], "row", n_row, lead)
+    far = swap(grad, "row", n_row, second)
+    left = swap(pairs_of(grad, cut(own, 1)), "row", n_row, first)
+    right = swap(pairs_of(far, cut(near, 1)), "row", n_row, first)
+    grad = grad + far + cut(left, 0) + cut(right, 0)
+    filtered = cut(own, 1) + cut(near, 1) + cut(left, 1) + cut(right, 1)
+    grad_blocks, filtered_blocks = across_cores([grad, filtered], n_row)
     purified, back, scaled_rows = purify_step(both, kept, masked_cols, both_held)
-    return last_step(kept, purified, back, pair_rows, scaled_rows, late_held)
+    return last_step(kept, purified, back, pair_rows, scaled_rows, grad_blocks, filtered_blocks)
 
 
 def solution(mesh):

time: 35.5 us -> 35.6 us (level)
  waiting for transfers between devices: 13.3 us -> 14.6 us
  starting transfers between devices: 18.4 us -> 17.1 us
    ppermute x14 -> x12, starting transfers between devices: 18.4 us -> 17 us  [swap(): lax.ppermute(blocks, axis_name, [(i, i ^ flip) for i in range(size)])]
    ppermute x14 -> x12, waiting for transfers between devices: 13.3 us -> 14.2 us  [swap(): lax.ppermute(blocks, axis_name, [(i, i ^ flip) for i in range(size)])]
    ppermute x0 -> x2, waiting for transfers between devices: none -> 0.38 us  [across_cores(): lax.ppermute(sent, 'row', [(i, i ^ flip) for i in range(n_row)])]
  transfers between devices with their start and end apart: 14 -> 14, of which waited for: 7 -> 9; matrix products, arithmetic and copies ran while one was open for 0% -> 1% of each run, Pallas kernels for 1% -> 1%
where the time goes in v1:
time: 35.6 us; the launch traced here: 35.5 us
  starting transfers between devices  17.1 us (48%)
  waiting for transfers between devices  14.6 us (41%)
  Pallas kernels  2.73 us (8%)
  between operations  0.74 us (2%)
    ppermute x12, starting transfers between devices, swap(): lax.ppermute(blocks, axis_name, [(i, i ^ flip) for i in range(size)])  17 us
    ppermute x12, waiting for transfers between devices, swap(): lax.ppermute(blocks, axis_name, [(i, i ^ flip) for i in range(size)])  14.2 us
    pallas_call x3, Pallas kernels, call(): pl.pallas_call(body, out_shape=out_shape, in_specs=[IN_VMEM] * len(arrays...  1.78 us
    pallas_call x1, Pallas kernels, mask(): pl.pallas_call(kernel, out_shape=(pltpu.VMEM((2, height, width), density....  0.94 us
  transfers between devices with their start and end apart: 14, of which 9 were waited for; matrix products, arithmetic and copies ran while one was open for 1% of the time, Pallas kernels for 1%

profile of v1, /device:TPU:0, one launch (start us, length us, event | category | flops | bytes accessed | tf_op | source)
XLA Modules:
  0.0 35.5 jit_solution(13066618981010362986)
XLA Ops:
  0.6 0.9 %mask.1 = (bf16[2,128,256]{2,1,0:T(8,128)(2,1)S(1)}, f32[2,128,256]{2,1,0:T(8,128)S(1)}) custom-call(s32[2,4]{1,0:T(2,128)} %refs_0_.1, s32[2,4]{1,0:T(2,128)} %refs_1_.1, bf16[128,256]{1,0:T(8,128)(2,1)} %refs_2_.1, bf16[128,256]{1,0:T(8,128)(2,1)} %refs_3_.1), custom_call_target="tpu_custom_call" | custom-call | tf_op jit(solution)/shard_map/mask/pallas_call | solution.py:44
  1.6 4.1 %collective-permute-start.5 = (bf16[1,2,128,256]{3,2,1,0:T(8,128)(2,1)S(1)}, bf16[1,2,128,256]{3,2,1,0:T(8,128)(2,1)S(1)}, u32[]{:S(2)}, u32[]{:S(2)}) collective-permute-start(bf16[1,2,128,256]{3,2,1,0:T(8,128)(2,1)S(1)} %bitcast.27), channel_id=1, source_target_pairs={{0,2},{1,3},{2,0},{3,1},{4,6},{5,7},{6,4},{7,5},{8,10},{9,11},{10,... | collective-permute-start | bytes 393224 | tf_op jit(solution)/shard_map/ppermute | solution.py:86
  5.7 1.6 %collective-permute-start.4 = (bf16[1,2,128,256]{3,2,1,0:T(8,128)(2,1)S(1)}, bf16[1,2,128,256]{3,2,1,0:T(8,128)(2,1)S(1)}, u32[]{:S(2)}, u32[]{:S(2)}) collective-permute-start(bf16[1,2,128,256]{3,2,1,0:T(8,128)(2,1)S(1)} %bitcast.28), channel_id=1, source_target_pairs={{0,1},{1,0},{2,3},{3,2},{4,5},{5,4},{6,7},{7,6},{8,9},{9,8},{10,11... | collective-permute-start | bytes 393224 | tf_op jit(solution)/shard_map/ppermute | solution.py:86
  7.3 1.5 %collective-permute-start.1 = (bf16[1,2,128,256]{3,2,1,0:T(8,128)(2,1)S(1)}, bf16[1,2,128,256]{3,2,1,0:T(8,128)(2,1)S(1)}, u32[]{:S(2)}, u32[]{:S(2)}) collective-permute-start(bf16[1,2,128,256]{3,2,1,0:T(8,128)(2,1)S(1)} %bitcast.29), channel_id=1, source_target_pairs={{0,8},{4,12},{8,0},{12,4},{16,24},{20,28},{24,16},{28,20},{1,9},{5... | collective-permute-start | bytes 393224 | tf_op jit(solution)/shard_map/ppermute | solution.py:86
  8.8 1.6 %collective-permute-start = (bf16[1,128,256]{2,1,0:T(8,128)(2,1)S(1)}, bf16[1,128,256]{2,1,0:T(8,128)(2,1)S(1)}, u32[]{:S(2)}, u32[]{:S(2)}) collective-permute-start(bf16[1,128,256]{2,1,0:T(8,128)(2,1)S(1)} %get-tuple-element.28.refs_2_), channel_id=1, source_target_pairs={{0,16},{4,20},{8,24},{12,28},{16,0},{20,4},{24,8},{28,12},{1,17},{... | collective-permute-start | bytes 196616 | tf_op jit(solution)/shard_map/ppermute | solution.py:86
  10.3 2.7 %collective-permute-done.refs_3_ = bf16[1,128,256]{2,1,0:T(8,128)(2,1)S(1)} collective-permute-done((bf16[1,128,256]{2,1,0:T(8,128)(2,1)S(1)}, bf16[1,128,256]{2,1,0:T(8,128)(2,1)S(1)}, u32[]{:S(2)}, u32[]{:S(2)}) %collective-permute-start) | collective-permute-done | bytes 65568 | tf_op jit(solution)/shard_map/ppermute | solution.py:86
  13.1 0.5 %collective-permute-start.2 = (bf16[1,128,256]{2,1,0:T(8,128)(2,1)S(1)}, bf16[1,128,256]{2,1,0:T(8,128)(2,1)S(1)}, u32[]{:S(2)}, u32[]{:S(2)}) collective-permute-start(bf16[1,128,256]{2,1,0:T(8,128)(2,1)S(1)} %collective-permute-done.refs_3_), channel_id=1, source_target_pairs={{0,8},{4,12},{8,0},{12,4},{16,24},{20,28},{24,16},{28,20},{1,9},{5... | collective-permute-start | bytes 196616 | tf_op jit(solution)/shard_map/ppermute | solution.py:86
  13.6 0.5 %collective-permute-start.6 = (bf16[1,2,128,256]{3,2,1,0:T(8,128)(2,1)S(1)}, bf16[1,2,128,256]{3,2,1,0:T(8,128)(2,1)S(1)}, u32[]{:S(2)}, u32[]{:S(2)}) collective-permute-start(bf16[1,2,128,256]{3,2,1,0:T(8,128)(2,1)S(1)} %collective-permute-done.5.refs_8_), channel_id=1, source_target_pairs={{0,1},{1,0},{2,3},{3,2},{4,5},{5,4},{6,7},{7,6},{8,9},{9,8},{10,11... | collective-permute-start | bytes 393224 | tf_op jit(solution)/shard_map/ppermute | solution.py:86
  14.1 3.3 %collective-permute-done.2.refs_5_ = bf16[1,128,256]{2,1,0:T(8,128)(2,1)S(1)} collective-permute-done((bf16[1,128,256]{2,1,0:T(8,128)(2,1)S(1)}, bf16[1,128,256]{2,1,0:T(8,128)(2,1)S(1)}, u32[]{:S(2)}, u32[]{:S(2)}) %collective-permute-start.2) | collective-permute-done | bytes 65568 | tf_op jit(solution)/shard_map/ppermute | solution.py:86
  17.5 1.1 %collective-permute-done.6.block_ref = bf16[1,2,128,256]{3,2,1,0:T(8,128)(2,1)S(1)} collective-permute-done((bf16[1,2,128,256]{3,2,1,0:T(8,128)(2,1)S(1)}, bf16[1,2,128,256]{3,2,1,0:T(8,128)(2,1)S(1)}, u32[]{:S(2)}, u32[]{:S(2)}) %collective-permute-start.6) | collective-permute-done | bytes 131104 | tf_op jit(solution)/shard_map/ppermute | solution.py:86
  18.6 0.4 %collective-permute-done.3.refs_6_ = bf16[1,4,128,256]{3,2,1,0:T(8,128)(2,1)S(1)} collective-permute-done((bf16[1,4,128,256]{3,2,1,0:T(8,128)(2,1)S(1)}, bf16[1,4,128,256]{3,2,1,0:T(8,128)(2,1)S(1)}, u32[]{:S(2)}, u32[]{:S(2)}) %collective-permute-start.3) | collective-permute-done | bytes 262176 | tf_op jit(solution)/shard_map/ppermute | solution.py:263
  19.0 0.4 %square_step.1 = (bf16[2,128,256]{2,1,0:T(8,128)(2,1)S(1)}, bf16[1024,256]{1,0:T(8,128)(2,1)S(1)}, bf16[256,1024]{1,0:T(8,128)(2,1)S(1)}) custom-call(bf16[2,128,256]{2,1,0:T(8,128)(2,1)S(1)} %get-tuple-element.15.refs_0_, f32[2,128,256]{2,1,0:T(8,128)S(1)} %get-tuple-element.14.refs_1_.refs_0_, bf16[1,128,256]{2,1,0:T(8,128)(2,1)S(1)} %get-tuple-element.28.refs_2_, ...), custom_call_target="tpu_custom_call" | custom-call | tf_op jit(solution)/shard_map/square_step/pallas_call | solution.py:160
  19.4 0.9 %collective-permute-start.8 = (bf16[1,2,128,256]{3,2,1,0:T(8,128)(2,1)S(1)}, bf16[1,2,128,256]{3,2,1,0:T(8,128)(2,1)S(1)}, u32[]{:S(2)}, u32[]{:S(2)}) collective-permute-start(bf16[1,2,128,256]{3,2,1,0:T(8,128)(2,1)S(1)} %bitcast.33), channel_id=1, source_target_pairs={{0,2},{1,3},{2,0},{3,1},{4,6},{5,7},{6,4},{7,5},{8,10},{9,11},{10,... | collective-permute-start | bytes 393224 | tf_op jit(solution)/shard_map/ppermute | solution.py:86
  20.3 1.7 %collective-permute-start.7 = (bf16[1,2,128,256]{3,2,1,0:T(8,128)(2,1)S(1)}, bf16[1,2,128,256]{3,2,1,0:T(8,128)(2,1)S(1)}, u32[]{:S(2)}, u32[]{:S(2)}) collective-permute-start(bf16[1,2,128,256]{3,2,1,0:T(8,128)(2,1)S(1)} %bitcast.34), channel_id=1, source_target_pairs={{0,1},{1,0},{2,3},{3,2},{4,5},{5,4},{6,7},{7,6},{8,9},{9,8},{10,11... | collective-permute-start | bytes 393224 | tf_op jit(solution)/shard_map/ppermute | solution.py:86
  22.0 1.5 %collective-permute-start.10 = (bf16[1,128,256]{2,1,0:T(8,128)(2,1)S(1)}, bf16[1,128,256]{2,1,0:T(8,128)(2,1)S(1)}, u32[]{:S(2)}, u32[]{:S(2)}) collective-permute-start(bf16[1,128,256]{2,1,0:T(8,128)(2,1)S(1)} %get-tuple-element.37.refs_5_), channel_id=1, source_target_pairs={{0,8},{4,12},{8,0},{12,4},{16,24},{20,28},{24,16},{28,20},{1,9},{5... | collective-permute-start | bytes 196616 | tf_op jit(solution)/shard_map/ppermute | solution.py:86
  23.5 1.6 %collective-permute-start.11 = (bf16[1,2,128,256]{3,2,1,0:T(8,128)(2,1)S(1)}, bf16[1,2,128,256]{3,2,1,0:T(8,128)(2,1)S(1)}, u32[]{:S(2)}, u32[]{:S(2)}) collective-permute-start(bf16[1,2,128,256]{3,2,1,0:T(8,128)(2,1)S(1)} %pad_maximum_fusion.1), channel_id=1, source_target_pairs={{0,16},{4,20},{8,24},{12,28},{16,0},{20,4},{24,8},{28,12},{1,17},{... | collective-permute-start | bytes 393224 | tf_op jit(solution)/shard_map/ppermute | solution.py:86
  25.1 1.2 %collective-permute-done.10.refs_6_ = bf16[1,128,256]{2,1,0:T(8,128)(2,1)S(1)} collective-permute-done((bf16[1,128,256]{2,1,0:T(8,128)(2,1)S(1)}, bf16[1,128,256]{2,1,0:T(8,128)(2,1)S(1)}, u32[]{:S(2)}, u32[]{:S(2)}) %collective-permute-start.10) | collective-permute-done | bytes 65568 | tf_op jit(solution)/shard_map/ppermute | solution.py:86
  26.3 1.6 %collective-permute-start.12 = (bf16[1,2,128,256]{3,2,1,0:T(8,128)(2,1)S(1)}, bf16[1,2,128,256]{3,2,1,0:T(8,128)(2,1)S(1)}, u32[]{:S(2)}, u32[]{:S(2)}) collective-permute-start(bf16[1,2,128,256]{3,2,1,0:T(8,128)(2,1)S(1)} %pad_maximum_fusion.2), channel_id=1, source_target_pairs={{0,16},{4,20},{8,24},{12,28},{16,0},{20,4},{24,8},{28,12},{1,17},{... | collective-permute-start | bytes 393224 | tf_op jit(solution)/shard_map/ppermute | solution.py:86
  27.9 0.7 %collective-permute-done.8.refs_4_ = bf16[1,2,128,256]{3,2,1,0:T(8,128)(2,1)S(1)} collective-permute-done((bf16[1,2,128,256]{3,2,1,0:T(8,128)(2,1)S(1)}, bf16[1,2,128,256]{3,2,1,0:T(8,128)(2,1)S(1)}, u32[]{:S(2)}, u32[]{:S(2)}) %collective-permute-start.8) | collective-permute-done | bytes 131104 | tf_op jit(solution)/shard_map/ppermute | solution.py:86
  28.6 0.9 %collective-permute-done.11 = bf16[1,2,128,256]{3,2,1,0:T(8,128)(2,1)S(1)} collective-permute-done((bf16[1,2,128,256]{3,2,1,0:T(8,128)(2,1)S(1)}, bf16[1,2,128,256]{3,2,1,0:T(8,128)(2,1)S(1)}, u32[]{:S(2)}, u32[]{:S(2)}) %collective-permute-start.11) | collective-permute-done | bytes 131104 | tf_op jit(solution)/shard_map/ppermute | solution.py:86
  29.5 1.8 %collective-permute-done.12 = bf16[1,2,128,256]{3,2,1,0:T(8,128)(2,1)S(1)} collective-permute-done((bf16[1,2,128,256]{3,2,1,0:T(8,128)(2,1)S(1)}, bf16[1,2,128,256]{3,2,1,0:T(8,128)(2,1)S(1)}, u32[]{:S(2)}, u32[]{:S(2)}) %collective-permute-start.12) | collective-permute-done | bytes 131104 | tf_op jit(solution)/shard_map/ppermute | solution.py:86
  31.6 2.5 %collective-permute-done.9.refs_6_ = bf16[1,2,128,256]{3,2,1,0:T(8,128)(2,1)S(1)} collective-permute-done((bf16[1,2,128,256]{3,2,1,0:T(8,128)(2,1)S(1)}, bf16[1,2,128,256]{3,2,1,0:T(8,128)(2,1)S(1)}, u32[]{:S(2)}, u32[]{:S(2)}) %collective-permute-start.9) | collective-permute-done | bytes 131104 | tf_op jit(solution)/shard_map/ppermute | solution.py:86
  34.1 0.4 %purify_step.1 = (bf16[128,256]{1,0:T(8,128)(2,1)S(1)}, f32[128,256]{1,0:T(8,128)S(1)}, bf16[128,1024]{1,0:T(8,128)(2,1)S(1)}) custom-call(bf16[2,128,256]{2,1,0:T(8,128)(2,1)S(1)} %get-tuple-element.18.refs_0_, f32[2,128,256]{2,1,0:T(8,128)S(1)} %get-tuple-element.14.refs_1_.refs_0_, bf16[1024,256]{1,0:T(8,128)(2,1)S(1)} %get-tuple-element.19.refs_2_, ...), custom_call_target="tpu_custom_call" | custom-call | flops 6000000000 | tf_op jit(solution)/shard_map/purify_step/pallas_call | solution.py:160
  34.4 1.0 %last_step.1 = (bf16[128,256]{1,0:T(8,128)(2,1)}, bf16[128,256]{1,0:T(8,128)(2,1)}) custom-call(f32[2,128,256]{2,1,0:T(8,128)S(1)} %get-tuple-element.14.refs_1_.refs_0_, bf16[128,256]{1,0:T(8,128)(2,1)S(1)} %get-tuple-element.22.refs_1_, f32[128,256]{1,0:T(8,128)S(1)} %get-tuple-element.23.refs_2_, bf16[256,1024]{1,0:T(8,128)(2,1)S(1)} %get-tuple-element.24.refs_3_, ...), custom_call_target="tpu_custom_call" | custom-call | tf_op jit(solution)/shard_map/last_step/pallas_call | solution.py:160
  (19 shorter events, 0.4 us)
Async XLA Ops:
  1.6 12.1 %collective-permute-start.5 = (bf16[1,2,128,256]{3,2,1,0:T(8,128)(2,1)S(1)}, bf16[1,2,128,256]{3,2,1,0:T(8,128)(2,1)S(1)}, u32[]{:S(2)}, u32[]{:S(2)}) collective-permute-start(bf16[1,2,128,256]{3,2,1,0:T(8,128)(2,1)S(1)} %bitcast.27), channel_id=1, source_target_pairs={{0,2},{1,3},{2,0},{3,1},{4,6},{5,7},{6,4},{7,5},{8,10},{9,11},{10,... | collective-permute-start | bytes 393224 | tf_op jit(solution)/shard_map/ppermute | solution.py:86
  5.7 8.0 %collective-permute-start.4 = (bf16[1,2,128,256]{3,2,1,0:T(8,128)(2,1)S(1)}, bf16[1,2,128,256]{3,2,1,0:T(8,128)(2,1)S(1)}, u32[]{:S(2)}, u32[]{:S(2)}) collective-permute-start(bf16[1,2,128,256]{3,2,1,0:T(8,128)(2,1)S(1)} %bitcast.28), channel_id=1, source_target_pairs={{0,1},{1,0},{2,3},{3,2},{4,5},{5,4},{6,7},{7,6},{8,9},{9,8},{10,11... | collective-permute-start | bytes 393224 | tf_op jit(solution)/shard_map/ppermute | solution.py:86
  7.3 6.8 %collective-permute-start.1 = (bf16[1,2,128,256]{3,2,1,0:T(8,128)(2,1)S(1)}, bf16[1,2,128,256]{3,2,1,0:T(8,128)(2,1)S(1)}, u32[]{:S(2)}, u32[]{:S(2)}) collective-permute-start(bf16[1,2,128,256]{3,2,1,0:T(8,128)(2,1)S(1)} %bitcast.29), channel_id=1, source_target_pairs={{0,8},{4,12},{8,0},{12,4},{16,24},{20,28},{24,16},{28,20},{1,9},{5... | collective-permute-start | bytes 393224 | tf_op jit(solution)/shard_map/ppermute | solution.py:86
  8.8 4.3 %collective-permute-start = (bf16[1,128,256]{2,1,0:T(8,128)(2,1)S(1)}, bf16[1,128,256]{2,1,0:T(8,128)(2,1)S(1)}, u32[]{:S(2)}, u32[]{:S(2)}) collective-permute-start(bf16[1,128,256]{2,1,0:T(8,128)(2,1)S(1)} %get-tuple-element.28.refs_2_), channel_id=1, source_target_pairs={{0,16},{4,20},{8,24},{12,28},{16,0},{20,4},{24,8},{28,12},{1,17},{... | collective-permute-start | bytes 196616 | tf_op jit(solution)/shard_map/ppermute | solution.py:86
  13.1 4.3 %collective-permute-start.2 = (bf16[1,128,256]{2,1,0:T(8,128)(2,1)S(1)}, bf16[1,128,256]{2,1,0:T(8,128)(2,1)S(1)}, u32[]{:S(2)}, u32[]{:S(2)}) collective-permute-start(bf16[1,128,256]{2,1,0:T(8,128)(2,1)S(1)} %collective-permute-done.refs_3_), channel_id=1, source_target_pairs={{0,8},{4,12},{8,0},{12,4},{16,24},{20,28},{24,16},{28,20},{1,9},{5... | collective-permute-start | bytes 196616 | tf_op jit(solution)/shard_map/ppermute | solution.py:86
  13.6 5.0 %collective-permute-start.6 = (bf16[1,2,128,256]{3,2,1,0:T(8,128)(2,1)S(1)}, bf16[1,2,128,256]{3,2,1,0:T(8,128)(2,1)S(1)}, u32[]{:S(2)}, u32[]{:S(2)}) collective-permute-start(bf16[1,2,128,256]{3,2,1,0:T(8,128)(2,1)S(1)} %collective-permute-done.5.refs_8_), channel_id=1, source_target_pairs={{0,1},{1,0},{2,3},{3,2},{4,5},{5,4},{6,7},{7,6},{8,9},{9,8},{10,11... | collective-permute-start | bytes 393224 | tf_op jit(solution)/shard_map/ppermute | solution.py:86
  17.4 1.6 %collective-permute-start.3 = (bf16[1,4,128,256]{3,2,1,0:T(8,128)(2,1)S(1)}, bf16[1,4,128,256]{3,2,1,0:T(8,128)(2,1)S(1)}, u32[]{:S(2)}, u32[]{:S(2)}) collective-permute-start(bf16[1,4,128,256]{3,2,1,0:T(8,128)(2,1)S(1)} %maximum_bitcast_fusion), channel_id=1, source_target_pairs={{0,4},{4,0},{8,12},{12,8},{16,20},{20,16},{24,28},{28,24},{1,5},{5... | collective-permute-start | bytes 786440 | tf_op jit(solution)/shard_map/ppermute | solution.py:263
  19.4 9.2 %collective-permute-start.8 = (bf16[1,2,128,256]{3,2,1,0:T(8,128)(2,1)S(1)}, bf16[1,2,128,256]{3,2,1,0:T(8,128)(2,1)S(1)}, u32[]{:S(2)}, u32[]{:S(2)}) collective-permute-start(bf16[1,2,128,256]{3,2,1,0:T(8,128)(2,1)S(1)} %bitcast.33), channel_id=1, source_target_pairs={{0,2},{1,3},{2,0},{3,1},{4,6},{5,7},{6,4},{7,5},{8,10},{9,11},{10,... | collective-permute-start | bytes 393224 | tf_op jit(solution)/shard_map/ppermute | solution.py:86
  20.3 8.3 %collective-permute-start.7 = (bf16[1,2,128,256]{3,2,1,0:T(8,128)(2,1)S(1)}, bf16[1,2,128,256]{3,2,1,0:T(8,128)(2,1)S(1)}, u32[]{:S(2)}, u32[]{:S(2)}) collective-permute-start(bf16[1,2,128,256]{3,2,1,0:T(8,128)(2,1)S(1)} %bitcast.34), channel_id=1, source_target_pairs={{0,1},{1,0},{2,3},{3,2},{4,5},{5,4},{6,7},{7,6},{8,9},{9,8},{10,11... | collective-permute-start | bytes 393224 | tf_op jit(solution)/shard_map/ppermute | solution.py:86
  22.0 4.3 %collective-permute-start.10 = (bf16[1,128,256]{2,1,0:T(8,128)(2,1)S(1)}, bf16[1,128,256]{2,1,0:T(8,128)(2,1)S(1)}, u32[]{:S(2)}, u32[]{:S(2)}) collective-permute-start(bf16[1,128,256]{2,1,0:T(8,128)(2,1)S(1)} %get-tuple-element.37.refs_5_), channel_id=1, source_target_pairs={{0,8},{4,12},{8,0},{12,4},{16,24},{20,28},{24,16},{28,20},{1,9},{5... | collective-permute-start | bytes 196616 | tf_op jit(solution)/shard_map/ppermute | solution.py:86
  23.5 6.0 %collective-permute-start.11 = (bf16[1,2,128,256]{3,2,1,0:T(8,128)(2,1)S(1)}, bf16[1,2,128,256]{3,2,1,0:T(8,128)(2,1)S(1)}, u32[]{:S(2)}, u32[]{:S(2)}) collective-permute-start(bf16[1,2,128,256]{3,2,1,0:T(8,128)(2,1)S(1)} %pad_maximum_fusion.1), channel_id=1, source_target_pairs={{0,16},{4,20},{8,24},{12,28},{16,0},{20,4},{24,8},{28,12},{1,17},{... | collective-permute-start | bytes 393224 | tf_op jit(solution)/shard_map/ppermute | solution.py:86
  26.3 5.0 %collective-permute-start.12 = (bf16[1,2,128,256]{3,2,1,0:T(8,128)(2,1)S(1)}, bf16[1,2,128,256]{3,2,1,0:T(8,128)(2,1)S(1)}, u32[]{:S(2)}, u32[]{:S(2)}) collective-permute-start(bf16[1,2,128,256]{3,2,1,0:T(8,128)(2,1)S(1)} %pad_maximum_fusion.2), channel_id=1, source_target_pairs={{0,16},{4,20},{8,24},{12,28},{16,0},{20,4},{24,8},{28,12},{1,17},{... | collective-permute-start | bytes 393224 | tf_op jit(solution)/shard_map/ppermute | solution.py:86
  28.6 5.4 %collective-permute-start.9 = (bf16[1,2,128,256]{3,2,1,0:T(8,128)(2,1)S(1)}, bf16[1,2,128,256]{3,2,1,0:T(8,128)(2,1)S(1)}, u32[]{:S(2)}, u32[]{:S(2)}) collective-permute-start(bf16[1,2,128,256]{3,2,1,0:T(8,128)(2,1)S(1)} %collective-permute-done.8.refs_4_), channel_id=1, source_target_pairs={{0,1},{1,0},{2,3},{3,2},{4,5},{5,4},{6,7},{7,6},{8,9},{9,8},{10,11... | collective-permute-start | bytes 393224 | tf_op jit(solution)/shard_map/ppermute | solution.py:86
  31.5 2.9 %collective-permute-start.13 = (bf16[2,4,128,256]{3,2,1,0:T(8,128)(2,1)S(1)}, bf16[2,4,128,256]{3,2,1,0:T(8,128)(2,1)S(1)}, u32[]{:S(2)}, u32[]{:S(2)}) collective-permute-start(bf16[2,4,128,256]{3,2,1,0:T(8,128)(2,1)S(1)} %pad_maximum_fusion), channel_id=1, source_target_pairs={{0,4},{4,0},{8,12},{12,8},{16,20},{20,16},{24,28},{28,24},{1,5},{5... | collective-permute-start | bytes 1572872 | tf_op jit(solution)/shard_map/ppermute | solution.py:263

commit v2 on v1

--- a/solution.py
+++ b/solution.py
@@ -109,17 +109,18 @@
     return [[(ats, block) for (ats, _), block in zip(held, blocks)] for held, blocks in zip(helds, arrays)]
 
 
-def exchange(pair, axis_name, size, settled):
+def exchange(pair, axis_name, size, settled, later=()):
     flips = flips_of(size)
     held = double([([0], pair[None])], axis_name, size, flips[:-2])
     far = swap(held, axis_name, size, flips[-2:-1])
     near = swap(held, axis_name, size, flips[-1:])
     near, far = tie([near, far])
+    _, later = tie([far, later])
     last = swap(far, axis_name, size, flips[-1:])
     if settled:
         last = [(ats, settle(pairs)) for ats, pairs in last]
     held = held + far + near + last
-    return [(at, ((pairs, (k, 0)), (pairs, (k, 1)))) for ats, pairs in held for k, at in enumerate(ats)]
+    return [(at, ((pairs, (k, 0)), (pairs, (k, 1)))) for ats, pairs in held for k, at in enumerate(ats)], later
 
 
 def part(ref, owner, size):
@@ -272,22 +273,23 @@
     lead, first, second = chip_flips[:-2], chip_flips[-2:-1], chip_flips[-1:]
     pair, kept = mask(density, cotangent, block_pattern, filter_pattern)
 
-    pair_held = exchange(pair, "col", n_col, True)
     own = double([([0], pair[None])], "row", n_row, lead)
-    masked = cut(own, 0)
+    masked, filtered = cut(own, 0), cut(own, 1)
+    pair_held, later = exchange(pair, "col", n_col, True, filtered)
     far = swap(masked, "row", n_row, first)
-    near = swap(own, "row", n_row, second)
-    masked = masked + far + cut(near, 0) + swap(far, "row", n_row, second)
+    near = swap(masked, "row", n_row, second)
+    masked = masked + far + near + swap(far, "row", n_row, second)
+    other = swap(later, "row", n_row, second)
     (masked_blocks,) = across_cores([masked], n_row)
     both, masked_cols, pair_rows = square_step(pair, kept, masked_blocks, pair_held)
 
-    both_held = exchange(both, "col", n_col, False)
+    both_held, _ = exchange(both, "col", n_col, False)
     grad = double([([0], both[1:])], "row", n_row, lead)
     far = swap(grad, "row", n_row, second)
-    left = swap(pairs_of(grad, cut(own, 1)), "row", n_row, first)
-    right = swap(pairs_of(far, cut(near, 1)), "row", n_row, first)
+    left = swap(pairs_of(grad, filtered), "row", n_row, first)
+    right = swap(pairs_of(far, other), "row", n_row, first)
     grad = grad + far + cut(left, 0) + cut(right, 0)
-    filtered = cut(own, 1) + cut(near, 1) + cut(left, 1) + cut(right, 1)
+    filtered = filtered + other + cut(left, 1) + cut(right, 1)
     grad_blocks, filtered_blocks = across_cores([grad, filtered], n_row)
     purified, back, scaled_rows = purify_step(both, kept, masked_cols, both_held)
     return last_step(kept, purified, back, pair_rows, scaled_rows, grad_blocks, filtered_blocks)

time: 35.6 us -> 34.9 us (0.980)
  waiting for transfers between devices: 14.6 us -> 10.1 us
  starting transfers between devices: 17.1 us -> 20.9 us
    ppermute x12 -> x13, waiting for transfers between devices: 14.2 us -> 10.1 us  [swap(): lax.ppermute(blocks, axis_name, [(i, i ^ flip) for i in range(size)])]
    ppermute x12 -> x13, starting transfers between devices: 17 us -> 20.7 us  [swap(): lax.ppermute(blocks, axis_name, [(i, i ^ flip) for i in range(size)])]
    ppermute x2, waiting for transfers between devices: 0.38 us -> 0.01 us  [across_cores(): lax.ppermute(sent, 'row', [(i, i ^ flip) for i in range(n_row)])]
  transfers between devices with their start and end apart: 14 -> 15, of which waited for: 9 -> 8; matrix products, arithmetic and copies ran while one was open for 1% -> 1% of each run, Pallas kernels for 1% -> 2%
where the time goes in v2:
time: 34.9 us; the launch traced here: 34.7 us
  starting transfers between devices  20.9 us (60%)
  waiting for transfers between devices  10.1 us (29%)
  Pallas kernels  2.74 us (8%)
  between operations  0.75 us (2%)
    ppermute x13, starting transfers between devices, swap(): lax.ppermute(blocks, axis_name, [(i, i ^ flip) for i in range(size)])  20.7 us
    ppermute x13, waiting for transfers between devices, swap(): lax.ppermute(blocks, axis_name, [(i, i ^ flip) for i in range(size)])  10.1 us
    pallas_call x3, Pallas kernels, call(): pl.pallas_call(body, out_shape=out_shape, in_specs=[IN_VMEM] * len(arrays...  1.79 us
    pallas_call x1, Pallas kernels, mask(): pl.pallas_call(kernel, out_shape=(pltpu.VMEM((2, height, width), density....  0.94 us
  transfers between devices with their start and end apart: 15, of which 8 were waited for; matrix products, arithmetic and copies ran while one was open for 1% of the time, Pallas kernels for 2%

profile of v2, /device:TPU:0, one launch (start us, length us, event | category | flops | bytes accessed | tf_op | source)
XLA Modules:
  0.0 34.7 jit_solution(275981651053507874)
XLA Ops:
  0.6 0.9 %mask.1 = (bf16[2,128,256]{2,1,0:T(8,128)(2,1)S(1)}, f32[2,128,256]{2,1,0:T(8,128)S(1)}) custom-call(s32[2,4]{1,0:T(2,128)} %refs_0_.1, s32[2,4]{1,0:T(2,128)} %refs_1_.1, bf16[128,256]{1,0:T(8,128)(2,1)} %refs_2_.1, bf16[128,256]{1,0:T(8,128)(2,1)} %refs_3_.1), custom_call_target="tpu_custom_call" | custom-call | tf_op jit(solution)/shard_map/mask/pallas_call | solution.py:44
  1.6 4.1 %collective-permute-start.5 = (bf16[1,2,128,256]{3,2,1,0:T(8,128)(2,1)S(1)}, bf16[1,2,128,256]{3,2,1,0:T(8,128)(2,1)S(1)}, u32[]{:S(2)}, u32[]{:S(2)}) collective-permute-start(bf16[1,2,128,256]{3,2,1,0:T(8,128)(2,1)S(1)} %bitcast.24), channel_id=1, source_target_pairs={{0,2},{1,3},{2,0},{3,1},{4,6},{5,7},{6,4},{7,5},{8,10},{9,11},{10,... | collective-permute-start | bytes 393224 | tf_op jit(solution)/shard_map/ppermute | solution.py:86
  5.7 1.6 %collective-permute-start.4 = (bf16[1,2,128,256]{3,2,1,0:T(8,128)(2,1)S(1)}, bf16[1,2,128,256]{3,2,1,0:T(8,128)(2,1)S(1)}, u32[]{:S(2)}, u32[]{:S(2)}) collective-permute-start(bf16[1,2,128,256]{3,2,1,0:T(8,128)(2,1)S(1)} %bitcast.25), channel_id=1, source_target_pairs={{0,1},{1,0},{2,3},{3,2},{4,5},{5,4},{6,7},{7,6},{8,9},{9,8},{10,11... | collective-permute-start | bytes 393224 | tf_op jit(solution)/shard_map/ppermute | solution.py:86
  7.3 1.6 %collective-permute-start = (bf16[1,128,256]{2,1,0:T(8,128)(2,1)S(1)}, bf16[1,128,256]{2,1,0:T(8,128)(2,1)S(1)}, u32[]{:S(2)}, u32[]{:S(2)}) collective-permute-start(bf16[1,128,256]{2,1,0:T(8,128)(2,1)S(1)} %get-tuple-element.34.refs_2_), channel_id=1, source_target_pairs={{0,16},{4,20},{8,24},{12,28},{16,0},{20,4},{24,8},{28,12},{1,17},{... | collective-permute-start | bytes 196616 | tf_op jit(solution)/shard_map/ppermute | solution.py:86
  8.9 1.5 %collective-permute-start.1 = (bf16[1,128,256]{2,1,0:T(8,128)(2,1)S(1)}, bf16[1,128,256]{2,1,0:T(8,128)(2,1)S(1)}, u32[]{:S(2)}, u32[]{:S(2)}) collective-permute-start(bf16[1,128,256]{2,1,0:T(8,128)(2,1)S(1)} %get-tuple-element.34.refs_2_), channel_id=1, source_target_pairs={{0,8},{4,12},{8,0},{12,4},{16,24},{20,28},{24,16},{28,20},{1,9},{5... | collective-permute-start | bytes 196616 | tf_op jit(solution)/shard_map/ppermute | solution.py:86
  10.3 1.3 %collective-permute-done.refs_3_ = bf16[1,128,256]{2,1,0:T(8,128)(2,1)S(1)} collective-permute-done((bf16[1,128,256]{2,1,0:T(8,128)(2,1)S(1)}, bf16[1,128,256]{2,1,0:T(8,128)(2,1)S(1)}, u32[]{:S(2)}, u32[]{:S(2)}) %collective-permute-start) | collective-permute-done | bytes 65568 | tf_op jit(solution)/shard_map/ppermute | solution.py:86
  11.6 1.5 %collective-permute-start.2 = (bf16[1,128,256]{2,1,0:T(8,128)(2,1)S(1)}, bf16[1,128,256]{2,1,0:T(8,128)(2,1)S(1)}, u32[]{:S(2)}, u32[]{:S(2)}) collective-permute-start(bf16[1,128,256]{2,1,0:T(8,128)(2,1)S(1)} %collective-permute-done.refs_3_), channel_id=1, source_target_pairs={{0,8},{4,12},{8,0},{12,4},{16,24},{20,28},{24,16},{28,20},{1,9},{5... | collective-permute-start | bytes 196616 | tf_op jit(solution)/shard_map/ppermute | solution.py:86
  13.1 0.6 %collective-permute-start.6 = (bf16[1,2,128,256]{3,2,1,0:T(8,128)(2,1)S(1)}, bf16[1,2,128,256]{3,2,1,0:T(8,128)(2,1)S(1)}, u32[]{:S(2)}, u32[]{:S(2)}) collective-permute-start(bf16[1,2,128,256]{3,2,1,0:T(8,128)(2,1)S(1)} %collective-permute-done.5.refs_8_), channel_id=1, source_target_pairs={{0,1},{1,0},{2,3},{3,2},{4,5},{5,4},{6,7},{7,6},{8,9},{9,8},{10,11... | collective-permute-start | bytes 393224 | tf_op jit(solution)/shard_map/ppermute | solution.py:86
  13.7 1.5 %collective-permute-start.12 = (bf16[1,128,256]{2,1,0:T(8,128)(2,1)S(1)}, bf16[1,128,256]{2,1,0:T(8,128)(2,1)S(1)}, u32[]{:S(2)}, u32[]{:S(2)}) collective-permute-start(bf16[1,128,256]{2,1,0:T(8,128)(2,1)S(1)} %get-tuple-element.27.refs_10_), channel_id=1, source_target_pairs={{0,8},{4,12},{8,0},{12,4},{16,24},{20,28},{24,16},{28,20},{1,9},{5... | collective-permute-start | bytes 196616 | tf_op jit(solution)/shard_map/ppermute | solution.py:86
  15.2 1.2 %collective-permute-done.2.refs_5_ = bf16[1,128,256]{2,1,0:T(8,128)(2,1)S(1)} collective-permute-done((bf16[1,128,256]{2,1,0:T(8,128)(2,1)S(1)}, bf16[1,128,256]{2,1,0:T(8,128)(2,1)S(1)}, u32[]{:S(2)}, u32[]{:S(2)}) %collective-permute-start.2) | collective-permute-done | bytes 65568 | tf_op jit(solution)/shard_map/ppermute | solution.py:86
  16.6 1.5 %collective-permute-done.6.block_ref = bf16[1,2,128,256]{3,2,1,0:T(8,128)(2,1)S(1)} collective-permute-done((bf16[1,2,128,256]{3,2,1,0:T(8,128)(2,1)S(1)}, bf16[1,2,128,256]{3,2,1,0:T(8,128)(2,1)S(1)}, u32[]{:S(2)}, u32[]{:S(2)}) %collective-permute-start.6) | collective-permute-done | bytes 131104 | tf_op jit(solution)/shard_map/ppermute | solution.py:86
  18.1 0.4 %square_step.1 = (bf16[2,128,256]{2,1,0:T(8,128)(2,1)S(1)}, bf16[1024,256]{1,0:T(8,128)(2,1)S(1)}, bf16[256,1024]{1,0:T(8,128)(2,1)S(1)}) custom-call(bf16[2,128,256]{2,1,0:T(8,128)(2,1)S(1)} %get-tuple-element.16.refs_0_, f32[2,128,256]{2,1,0:T(8,128)S(1)} %get-tuple-element.15.refs_1_.refs_0_, bf16[1,128,256]{2,1,0:T(8,128)(2,1)S(1)} %get-tuple-element.34.refs_2_, ...), custom_call_target="tpu_custom_call" | custom-call | tf_op jit(solution)/shard_map/square_step/pallas_call | solution.py:161
  18.5 1.8 %collective-permute-start.8 = (bf16[1,2,128,256]{3,2,1,0:T(8,128)(2,1)S(1)}, bf16[1,2,128,256]{3,2,1,0:T(8,128)(2,1)S(1)}, u32[]{:S(2)}, u32[]{:S(2)}) collective-permute-start(bf16[1,2,128,256]{3,2,1,0:T(8,128)(2,1)S(1)} %bitcast.30), channel_id=1, source_target_pairs={{0,2},{1,3},{2,0},{3,1},{4,6},{5,7},{6,4},{7,5},{8,10},{9,11},{10,... | collective-permute-start | bytes 393224 | tf_op jit(solution)/shard_map/ppermute | solution.py:86
  20.3 1.7 %collective-permute-start.7 = (bf16[1,2,128,256]{3,2,1,0:T(8,128)(2,1)S(1)}, bf16[1,2,128,256]{3,2,1,0:T(8,128)(2,1)S(1)}, u32[]{:S(2)}, u32[]{:S(2)}) collective-permute-start(bf16[1,2,128,256]{3,2,1,0:T(8,128)(2,1)S(1)} %bitcast.31), channel_id=1, source_target_pairs={{0,1},{1,0},{2,3},{3,2},{4,5},{5,4},{6,7},{7,6},{8,9},{9,8},{10,11... | collective-permute-start | bytes 393224 | tf_op jit(solution)/shard_map/ppermute | solution.py:86
  22.0 1.5 %collective-permute-start.10 = (bf16[1,128,256]{2,1,0:T(8,128)(2,1)S(1)}, bf16[1,128,256]{2,1,0:T(8,128)(2,1)S(1)}, u32[]{:S(2)}, u32[]{:S(2)}) collective-permute-start(bf16[1,128,256]{2,1,0:T(8,128)(2,1)S(1)} %get-tuple-element.36.refs_5_), channel_id=1, source_target_pairs={{0,8},{4,12},{8,0},{12,4},{16,24},{20,28},{24,16},{28,20},{1,9},{5... | collective-permute-start | bytes 196616 | tf_op jit(solution)/shard_map/ppermute | solution.py:86
  23.5 1.6 %collective-permute-start.11 = (bf16[1,2,128,256]{3,2,1,0:T(8,128)(2,1)S(1)}, bf16[1,2,128,256]{3,2,1,0:T(8,128)(2,1)S(1)}, u32[]{:S(2)}, u32[]{:S(2)}) collective-permute-start(bf16[1,2,128,256]{3,2,1,0:T(8,128)(2,1)S(1)} %pad_maximum_fusion.1), channel_id=1, source_target_pairs={{0,16},{4,20},{8,24},{12,28},{16,0},{20,4},{24,8},{28,12},{1,17},{... | collective-permute-start | bytes 393224 | tf_op jit(solution)/shard_map/ppermute | solution.py:86
  25.1 1.2 %collective-permute-done.10.refs_6_ = bf16[1,128,256]{2,1,0:T(8,128)(2,1)S(1)} collective-permute-done((bf16[1,128,256]{2,1,0:T(8,128)(2,1)S(1)}, bf16[1,128,256]{2,1,0:T(8,128)(2,1)S(1)}, u32[]{:S(2)}, u32[]{:S(2)}) %collective-permute-start.10) | collective-permute-done | bytes 65568 | tf_op jit(solution)/shard_map/ppermute | solution.py:86
  26.3 1.6 %collective-permute-start.13 = (bf16[1,2,128,256]{3,2,1,0:T(8,128)(2,1)S(1)}, bf16[1,2,128,256]{3,2,1,0:T(8,128)(2,1)S(1)}, u32[]{:S(2)}, u32[]{:S(2)}) collective-permute-start(bf16[1,2,128,256]{3,2,1,0:T(8,128)(2,1)S(1)} %pad_maximum_fusion.2), channel_id=1, source_target_pairs={{0,16},{4,20},{8,24},{12,28},{16,0},{20,4},{24,8},{28,12},{1,17},{... | collective-permute-start | bytes 393224 | tf_op jit(solution)/shard_map/ppermute | solution.py:86
  28.0 0.2 collective-permute-start.9
  28.2 1.3 %collective-permute-done.11 = bf16[1,2,128,256]{3,2,1,0:T(8,128)(2,1)S(1)} collective-permute-done((bf16[1,2,128,256]{3,2,1,0:T(8,128)(2,1)S(1)}, bf16[1,2,128,256]{3,2,1,0:T(8,128)(2,1)S(1)}, u32[]{:S(2)}, u32[]{:S(2)}) %collective-permute-start.11) | collective-permute-done | bytes 131104 | tf_op jit(solution)/shard_map/ppermute | solution.py:86
  29.5 1.8 %collective-permute-done.13 = bf16[1,2,128,256]{3,2,1,0:T(8,128)(2,1)S(1)} collective-permute-done((bf16[1,2,128,256]{3,2,1,0:T(8,128)(2,1)S(1)}, bf16[1,2,128,256]{3,2,1,0:T(8,128)(2,1)S(1)}, u32[]{:S(2)}, u32[]{:S(2)}) %collective-permute-start.13) | collective-permute-done | bytes 131104 | tf_op jit(solution)/shard_map/ppermute | solution.py:86
  31.6 1.7 %collective-permute-done.9.refs_6_ = bf16[1,2,128,256]{3,2,1,0:T(8,128)(2,1)S(1)} collective-permute-done((bf16[1,2,128,256]{3,2,1,0:T(8,128)(2,1)S(1)}, bf16[1,2,128,256]{3,2,1,0:T(8,128)(2,1)S(1)}, u32[]{:S(2)}, u32[]{:S(2)}) %collective-permute-start.9) | collective-permute-done | bytes 131104 | tf_op jit(solution)/shard_map/ppermute | solution.py:86
  33.3 0.4 %purify_step.1 = (bf16[128,256]{1,0:T(8,128)(2,1)S(1)}, f32[128,256]{1,0:T(8,128)S(1)}, bf16[128,1024]{1,0:T(8,128)(2,1)S(1)}) custom-call(bf16[2,128,256]{2,1,0:T(8,128)(2,1)S(1)} %get-tuple-element.19.refs_0_, f32[2,128,256]{2,1,0:T(8,128)S(1)} %get-tuple-element.15.refs_1_.refs_0_, bf16[1024,256]{1,0:T(8,128)(2,1)S(1)} %get-tuple-element.20.refs_2_, ...), custom_call_target="tpu_custom_call" | custom-call | flops 6000000000 | tf_op jit(solution)/shard_map/purify_step/pallas_call | solution.py:161
  33.7 1.0 %last_step.1 = (bf16[128,256]{1,0:T(8,128)(2,1)}, bf16[128,256]{1,0:T(8,128)(2,1)}) custom-call(f32[2,128,256]{2,1,0:T(8,128)S(1)} %get-tuple-element.15.refs_1_.refs_0_, bf16[128,256]{1,0:T(8,128)(2,1)S(1)} %get-tuple-element.23.refs_1_, f32[128,256]{1,0:T(8,128)S(1)} %get-tuple-element.24.refs_2_, bf16[256,1024]{1,0:T(8,128)(2,1)S(1)} %get-tuple-element.25.refs_3_, ...), custom_call_target="tpu_custom_call" | custom-call | tf_op jit(solution)/shard_map/last_step/pallas_call | solution.py:161
  (20 shorter events, 0.5 us)
Async XLA Ops:
  1.6 11.5 %collective-permute-start.5 = (bf16[1,2,128,256]{3,2,1,0:T(8,128)(2,1)S(1)}, bf16[1,2,128,256]{3,2,1,0:T(8,128)(2,1)S(1)}, u32[]{:S(2)}, u32[]{:S(2)}) collective-permute-start(bf16[1,2,128,256]{3,2,1,0:T(8,128)(2,1)S(1)} %bitcast.24), channel_id=1, source_target_pairs={{0,2},{1,3},{2,0},{3,1},{4,6},{5,7},{6,4},{7,5},{8,10},{9,11},{10,... | collective-permute-start | bytes 393224 | tf_op jit(solution)/shard_map/ppermute | solution.py:86
  5.7 7.4 %collective-permute-start.4 = (bf16[1,2,128,256]{3,2,1,0:T(8,128)(2,1)S(1)}, bf16[1,2,128,256]{3,2,1,0:T(8,128)(2,1)S(1)}, u32[]{:S(2)}, u32[]{:S(2)}) collective-permute-start(bf16[1,2,128,256]{3,2,1,0:T(8,128)(2,1)S(1)} %bitcast.25), channel_id=1, source_target_pairs={{0,1},{1,0},{2,3},{3,2},{4,5},{5,4},{6,7},{7,6},{8,9},{9,8},{10,11... | collective-permute-start | bytes 393224 | tf_op jit(solution)/shard_map/ppermute | solution.py:86
  7.3 4.3 %collective-permute-start = (bf16[1,128,256]{2,1,0:T(8,128)(2,1)S(1)}, bf16[1,128,256]{2,1,0:T(8,128)(2,1)S(1)}, u32[]{:S(2)}, u32[]{:S(2)}) collective-permute-start(bf16[1,128,256]{2,1,0:T(8,128)(2,1)S(1)} %get-tuple-element.34.refs_2_), channel_id=1, source_target_pairs={{0,16},{4,20},{8,24},{12,28},{16,0},{20,4},{24,8},{28,12},{1,17},{... | collective-permute-start | bytes 196616 | tf_op jit(solution)/shard_map/ppermute | solution.py:86
  8.9 6.4 %collective-permute-start.1 = (bf16[1,128,256]{2,1,0:T(8,128)(2,1)S(1)}, bf16[1,128,256]{2,1,0:T(8,128)(2,1)S(1)}, u32[]{:S(2)}, u32[]{:S(2)}) collective-permute-start(bf16[1,128,256]{2,1,0:T(8,128)(2,1)S(1)} %get-tuple-element.34.refs_2_), channel_id=1, source_target_pairs={{0,8},{4,12},{8,0},{12,4},{16,24},{20,28},{24,16},{28,20},{1,9},{5... | collective-permute-start | bytes 196616 | tf_op jit(solution)/shard_map/ppermute | solution.py:86
  11.6 4.8 %collective-permute-start.2 = (bf16[1,128,256]{2,1,0:T(8,128)(2,1)S(1)}, bf16[1,128,256]{2,1,0:T(8,128)(2,1)S(1)}, u32[]{:S(2)}, u32[]{:S(2)}) collective-permute-start(bf16[1,128,256]{2,1,0:T(8,128)(2,1)S(1)} %collective-permute-done.refs_3_), channel_id=1, source_target_pairs={{0,8},{4,12},{8,0},{12,4},{16,24},{20,28},{24,16},{28,20},{1,9},{5... | collective-permute-start | bytes 196616 | tf_op jit(solution)/shard_map/ppermute | solution.py:86
  13.1 5.0 %collective-permute-start.6 = (bf16[1,2,128,256]{3,2,1,0:T(8,128)(2,1)S(1)}, bf16[1,2,128,256]{3,2,1,0:T(8,128)(2,1)S(1)}, u32[]{:S(2)}, u32[]{:S(2)}) collective-permute-start(bf16[1,2,128,256]{3,2,1,0:T(8,128)(2,1)S(1)} %collective-permute-done.5.refs_8_), channel_id=1, source_target_pairs={{0,1},{1,0},{2,3},{3,2},{4,5},{5,4},{6,7},{7,6},{8,9},{9,8},{10,11... | collective-permute-start | bytes 393224 | tf_op jit(solution)/shard_map/ppermute | solution.py:86
  13.7 11.4 %collective-permute-start.12 = (bf16[1,128,256]{2,1,0:T(8,128)(2,1)S(1)}, bf16[1,128,256]{2,1,0:T(8,128)(2,1)S(1)}, u32[]{:S(2)}, u32[]{:S(2)}) collective-permute-start(bf16[1,128,256]{2,1,0:T(8,128)(2,1)S(1)} %get-tuple-element.27.refs_10_), channel_id=1, source_target_pairs={{0,8},{4,12},{8,0},{12,4},{16,24},{20,28},{24,16},{28,20},{1,9},{5... | collective-permute-start | bytes 196616 | tf_op jit(solution)/shard_map/ppermute | solution.py:86
  16.5 1.6 %collective-permute-start.3 = (bf16[1,4,128,256]{3,2,1,0:T(8,128)(2,1)S(1)}, bf16[1,4,128,256]{3,2,1,0:T(8,128)(2,1)S(1)}, u32[]{:S(2)}, u32[]{:S(2)}) collective-permute-start(bf16[1,4,128,256]{3,2,1,0:T(8,128)(2,1)S(1)} %maximum_bitcast_fusion), channel_id=1, source_target_pairs={{0,4},{4,0},{8,12},{12,8},{16,20},{20,16},{24,28},{28,24},{1,5},{5... | collective-permute-start | bytes 786440 | tf_op jit(solution)/shard_map/ppermute | solution.py:264
  18.5 9.4 %collective-permute-start.8 = (bf16[1,2,128,256]{3,2,1,0:T(8,128)(2,1)S(1)}, bf16[1,2,128,256]{3,2,1,0:T(8,128)(2,1)S(1)}, u32[]{:S(2)}, u32[]{:S(2)}) collective-permute-start(bf16[1,2,128,256]{3,2,1,0:T(8,128)(2,1)S(1)} %bitcast.30), channel_id=1, source_target_pairs={{0,2},{1,3},{2,0},{3,1},{4,6},{5,7},{6,4},{7,5},{8,10},{9,11},{10,... | collective-permute-start | bytes 393224 | tf_op jit(solution)/shard_map/ppermute | solution.py:86
  20.3 7.7 %collective-permute-start.7 = (bf16[1,2,128,256]{3,2,1,0:T(8,128)(2,1)S(1)}, bf16[1,2,128,256]{3,2,1,0:T(8,128)(2,1)S(1)}, u32[]{:S(2)}, u32[]{:S(2)}) collective-permute-start(bf16[1,2,128,256]{3,2,1,0:T(8,128)(2,1)S(1)} %bitcast.31), channel_id=1, source_target_pairs={{0,1},{1,0},{2,3},{3,2},{4,5},{5,4},{6,7},{7,6},{8,9},{9,8},{10,11... | collective-permute-start | bytes 393224 | tf_op jit(solution)/shard_map/ppermute | solution.py:86
  22.0 4.3 %collective-permute-start.10 = (bf16[1,128,256]{2,1,0:T(8,128)(2,1)S(1)}, bf16[1,128,256]{2,1,0:T(8,128)(2,1)S(1)}, u32[]{:S(2)}, u32[]{:S(2)}) collective-permute-start(bf16[1,128,256]{2,1,0:T(8,128)(2,1)S(1)} %get-tuple-element.36.refs_5_), channel_id=1, source_target_pairs={{0,8},{4,12},{8,0},{12,4},{16,24},{20,28},{24,16},{28,20},{1,9},{5... | collective-permute-start | bytes 196616 | tf_op jit(solution)/shard_map/ppermute | solution.py:86
  23.5 6.0 %collective-permute-start.11 = (bf16[1,2,128,256]{3,2,1,0:T(8,128)(2,1)S(1)}, bf16[1,2,128,256]{3,2,1,0:T(8,128)(2,1)S(1)}, u32[]{:S(2)}, u32[]{:S(2)}) collective-permute-start(bf16[1,2,128,256]{3,2,1,0:T(8,128)(2,1)S(1)} %pad_maximum_fusion.1), channel_id=1, source_target_pairs={{0,16},{4,20},{8,24},{12,28},{16,0},{20,4},{24,8},{28,12},{1,17},{... | collective-permute-start | bytes 393224 | tf_op jit(solution)/shard_map/ppermute | solution.py:86
  26.3 5.0 %collective-permute-start.13 = (bf16[1,2,128,256]{3,2,1,0:T(8,128)(2,1)S(1)}, bf16[1,2,128,256]{3,2,1,0:T(8,128)(2,1)S(1)}, u32[]{:S(2)}, u32[]{:S(2)}) collective-permute-start(bf16[1,2,128,256]{3,2,1,0:T(8,128)(2,1)S(1)} %pad_maximum_fusion.2), channel_id=1, source_target_pairs={{0,16},{4,20},{8,24},{12,28},{16,0},{20,4},{24,8},{28,12},{1,17},{... | collective-permute-start | bytes 393224 | tf_op jit(solution)/shard_map/ppermute | solution.py:86
  28.0 5.3 %collective-permute-start.9 = (bf16[1,2,128,256]{3,2,1,0:T(8,128)(2,1)S(1)}, bf16[1,2,128,256]{3,2,1,0:T(8,128)(2,1)S(1)}, u32[]{:S(2)}, u32[]{:S(2)}) collective-permute-start(bf16[1,2,128,256]{3,2,1,0:T(8,128)(2,1)S(1)} %collective-permute-done.8.refs_4_), channel_id=1, source_target_pairs={{0,1},{1,0},{2,3},{3,2},{4,5},{5,4},{6,7},{7,6},{8,9},{9,8},{10,11... | collective-permute-start | bytes 393224 | tf_op jit(solution)/shard_map/ppermute | solution.py:86
  31.5 2.2 %collective-permute-start.14 = (bf16[2,4,128,256]{3,2,1,0:T(8,128)(2,1)S(1)}, bf16[2,4,128,256]{3,2,1,0:T(8,128)(2,1)S(1)}, u32[]{:S(2)}, u32[]{:S(2)}) collective-permute-start(bf16[2,4,128,256]{3,2,1,0:T(8,128)(2,1)S(1)} %pad_maximum_fusion), channel_id=1, source_target_pairs={{0,4},{4,0},{8,12},{12,8},{16,20},{20,16},{24,28},{28,24},{1,5},{5... | collective-permute-start | bytes 1572872 | tf_op jit(solution)/shard_map/ppermute | solution.py:264

commit v3 on v2

--- a/solution.py
+++ b/solution.py
@@ -7,6 +7,7 @@
 
 IN_HBM = pl.BlockSpec(memory_space=pltpu.HBM)
 IN_VMEM = pl.BlockSpec(memory_space=pltpu.VMEM)
+SOON = pl.CostEstimate(flops=100_000_000, bytes_accessed=0, transcendentals=0)
 LIMIT = pltpu.CompilerParams(vmem_limit_bytes=32 * 1024 * 1024)
 EARLY = pl.CostEstimate(flops=6_000_000_000, bytes_accessed=0, transcendentals=0)
 
@@ -68,7 +69,7 @@
         out_shape=pltpu.VMEM(block.shape, block.dtype),
         in_specs=[IN_VMEM],
         out_specs=IN_VMEM,
-        cost_estimate=EARLY,
+        cost_estimate=hint,
         compiler_params=LIMIT,
         name="settle",
     )(block)
@@ -114,11 +115,14 @@
     held = double([([0], pair[None])], axis_name, size, flips[:-2])
     far = swap(held, axis_name, size, flips[-2:-1])
     near = swap(held, axis_name, size, flips[-1:])
-    near, far = tie([near, far])
     _, later = tie([far, later])
+    if settled:
+        near = [(ats, settle(pairs, SOON)) for ats, pairs in near]
+    else:
+        near, far = tie([near, far])
     last = swap(far, axis_name, size, flips[-1:])
     if settled:
-        last = [(ats, settle(pairs)) for ats, pairs in last]
+        last = [(ats, settle(pairs, EARLY)) for ats, pairs in last]
     held = held + far + near + last
     return [(at, ((pairs, (k, 0)), (pairs, (k, 1)))) for ats, pairs in held for k, at in enumerate(ats)], later
 
@@ -127,7 +131,7 @@
     return ref.at[pl.ds(pl.multiple_of(owner * size, size), size), :]
 
 
-def settle(block):
+def settle(block, hint):
     def kernel(block_ref, out_ref):
         out_ref[...] = block_ref[...]
 
@@ -136,7 +140,7 @@
         out_shape=pltpu.VMEM(block.shape, block.dtype),
         in_specs=[IN_VMEM],
         out_specs=IN_VMEM,
-        cost_estimate=EARLY,
+        cost_estimate=hint,
         compiler_params=LIMIT,
         name="settle",
     )(block)

time: 34.9 us -> 34.8 us (level)
  starting transfers between devices: 20.9 us -> 19.9 us
  waiting for transfers between devices: 10.1 us -> 11.1 us
    ppermute x13, starting transfers between devices: 20.7 us -> 19.7 us  [swap(): lax.ppermute(blocks, axis_name, [(i, i ^ flip) for i in range(size)])]
    ppermute x13, waiting for transfers between devices: 10.1 us -> 10.9 us  [swap(): lax.ppermute(blocks, axis_name, [(i, i ^ flip) for i in range(size)])]
where the time goes in v3:
time: 34.8 us; the launch traced here: 34.7 us
  starting transfers between devices  19.9 us (57%)
  waiting for transfers between devices  11.1 us (32%)
  Pallas kernels  2.74 us (8%)
  between operations  0.74 us (2%)
    ppermute x13, starting transfers between devices, swap(): lax.ppermute(blocks, axis_name, [(i, i ^ flip) for i in range(size)])  19.7 us
    ppermute x13, waiting for transfers between devices, swap(): lax.ppermute(blocks, axis_name, [(i, i ^ flip) for i in range(size)])  10.9 us
    pallas_call x3, Pallas kernels, call(): pl.pallas_call(body, out_shape=out_shape, in_specs=[IN_VMEM] * len(arrays...  1.78 us
    pallas_call x1, Pallas kernels, mask(): pl.pallas_call(kernel, out_shape=(pltpu.VMEM((2, height, width), density....  0.94 us
  transfers between devices with their start and end apart: 15, of which 8 were waited for; matrix products, arithmetic and copies ran while one was open for 1% of the time, Pallas kernels for 2%

profile of v3, /device:TPU:0, one launch (start us, length us, event | category | flops | bytes accessed | tf_op | source)
XLA Modules:
  0.0 34.7 jit_solution(5358082143504963694)
XLA Ops:
  0.6 0.9 %mask.1 = (bf16[2,128,256]{2,1,0:T(8,128)(2,1)S(1)}, f32[2,128,256]{2,1,0:T(8,128)S(1)}) custom-call(s32[2,4]{1,0:T(2,128)} %refs_0_.1, s32[2,4]{1,0:T(2,128)} %refs_1_.1, bf16[128,256]{1,0:T(8,128)(2,1)} %refs_2_.1, bf16[128,256]{1,0:T(8,128)(2,1)} %refs_3_.1), custom_call_target="tpu_custom_call" | custom-call | tf_op jit(solution)/shard_map/mask/pallas_call | solution.py:45
  1.6 4.1 %collective-permute-start.4 = (bf16[1,2,128,256]{3,2,1,0:T(8,128)(2,1)S(1)}, bf16[1,2,128,256]{3,2,1,0:T(8,128)(2,1)S(1)}, u32[]{:S(2)}, u32[]{:S(2)}) collective-permute-start(bf16[1,2,128,256]{3,2,1,0:T(8,128)(2,1)S(1)} %bitcast.24), channel_id=1, source_target_pairs={{0,2},{1,3},{2,0},{3,1},{4,6},{5,7},{6,4},{7,5},{8,10},{9,11},{10,... | collective-permute-start | bytes 393224 | tf_op jit(solution)/shard_map/ppermute | solution.py:87
  5.7 1.6 %collective-permute-start = (bf16[1,128,256]{2,1,0:T(8,128)(2,1)S(1)}, bf16[1,128,256]{2,1,0:T(8,128)(2,1)S(1)}, u32[]{:S(2)}, u32[]{:S(2)}) collective-permute-start(bf16[1,128,256]{2,1,0:T(8,128)(2,1)S(1)} %get-tuple-element.30.refs_2_), channel_id=1, source_target_pairs={{0,16},{4,20},{8,24},{12,28},{16,0},{20,4},{24,8},{28,12},{1,17},{... | collective-permute-start | bytes 196616 | tf_op jit(solution)/shard_map/ppermute | solution.py:87
  7.3 1.5 %collective-permute-start.1 = (bf16[1,128,256]{2,1,0:T(8,128)(2,1)S(1)}, bf16[1,128,256]{2,1,0:T(8,128)(2,1)S(1)}, u32[]{:S(2)}, u32[]{:S(2)}) collective-permute-start(bf16[1,128,256]{2,1,0:T(8,128)(2,1)S(1)} %get-tuple-element.30.refs_2_), channel_id=1, source_target_pairs={{0,8},{4,12},{8,0},{12,4},{16,24},{20,28},{24,16},{28,20},{1,9},{5... | collective-permute-start | bytes 196616 | tf_op jit(solution)/shard_map/ppermute | solution.py:87
  8.8 1.3 %collective-permute-done.refs_3_ = bf16[1,128,256]{2,1,0:T(8,128)(2,1)S(1)} collective-permute-done((bf16[1,128,256]{2,1,0:T(8,128)(2,1)S(1)}, bf16[1,128,256]{2,1,0:T(8,128)(2,1)S(1)}, u32[]{:S(2)}, u32[]{:S(2)}) %collective-permute-start) | collective-permute-done | bytes 65568 | tf_op jit(solution)/shard_map/ppermute | solution.py:87
  10.0 1.5 %collective-permute-start.2 = (bf16[1,128,256]{2,1,0:T(8,128)(2,1)S(1)}, bf16[1,128,256]{2,1,0:T(8,128)(2,1)S(1)}, u32[]{:S(2)}, u32[]{:S(2)}) collective-permute-start(bf16[1,128,256]{2,1,0:T(8,128)(2,1)S(1)} %collective-permute-done.refs_3_), channel_id=1, source_target_pairs={{0,8},{4,12},{8,0},{12,4},{16,24},{20,28},{24,16},{28,20},{1,9},{5... | collective-permute-start | bytes 196616 | tf_op jit(solution)/shard_map/ppermute | solution.py:87
  11.5 1.6 %collective-permute-start.5 = (bf16[1,2,128,256]{3,2,1,0:T(8,128)(2,1)S(1)}, bf16[1,2,128,256]{3,2,1,0:T(8,128)(2,1)S(1)}, u32[]{:S(2)}, u32[]{:S(2)}) collective-permute-start(bf16[1,2,128,256]{3,2,1,0:T(8,128)(2,1)S(1)} %bitcast.26), channel_id=1, source_target_pairs={{0,1},{1,0},{2,3},{3,2},{4,5},{5,4},{6,7},{7,6},{8,9},{9,8},{10,11... | collective-permute-start | bytes 393224 | tf_op jit(solution)/shard_map/ppermute | solution.py:87
  13.1 0.5 %collective-permute-start.6 = (bf16[1,2,128,256]{3,2,1,0:T(8,128)(2,1)S(1)}, bf16[1,2,128,256]{3,2,1,0:T(8,128)(2,1)S(1)}, u32[]{:S(2)}, u32[]{:S(2)}) collective-permute-start(bf16[1,2,128,256]{3,2,1,0:T(8,128)(2,1)S(1)} %collective-permute-done.4.refs_8_), channel_id=1, source_target_pairs={{0,1},{1,0},{2,3},{3,2},{4,5},{5,4},{6,7},{7,6},{8,9},{9,8},{10,11... | collective-permute-start | bytes 393224 | tf_op jit(solution)/shard_map/ppermute | solution.py:87
  13.6 0.7 %collective-permute-start.12 = (bf16[1,128,256]{2,1,0:T(8,128)(2,1)S(1)}, bf16[1,128,256]{2,1,0:T(8,128)(2,1)S(1)}, u32[]{:S(2)}, u32[]{:S(2)}) collective-permute-start(bf16[1,128,256]{2,1,0:T(8,128)(2,1)S(1)} %get-tuple-element.23.refs_10_), channel_id=1, source_target_pairs={{0,8},{4,12},{8,0},{12,4},{16,24},{20,28},{24,16},{28,20},{1,9},{5... | collective-permute-start | bytes 196616 | tf_op jit(solution)/shard_map/ppermute | solution.py:87
  14.4 2.3 %collective-permute-done.5.block_ref = bf16[1,2,128,256]{3,2,1,0:T(8,128)(2,1)S(1)} collective-permute-done((bf16[1,2,128,256]{3,2,1,0:T(8,128)(2,1)S(1)}, bf16[1,2,128,256]{3,2,1,0:T(8,128)(2,1)S(1)}, u32[]{:S(2)}, u32[]{:S(2)}) %collective-permute-start.5) | collective-permute-done | bytes 131104 | tf_op jit(solution)/shard_map/ppermute | solution.py:87
  16.7 1.4 %collective-permute-done.6.block_ref = bf16[1,2,128,256]{3,2,1,0:T(8,128)(2,1)S(1)} collective-permute-done((bf16[1,2,128,256]{3,2,1,0:T(8,128)(2,1)S(1)}, bf16[1,2,128,256]{3,2,1,0:T(8,128)(2,1)S(1)}, u32[]{:S(2)}, u32[]{:S(2)}) %collective-permute-start.6) | collective-permute-done | bytes 131104 | tf_op jit(solution)/shard_map/ppermute | solution.py:87
  18.1 0.4 %square_step.1 = (bf16[2,128,256]{2,1,0:T(8,128)(2,1)S(1)}, bf16[1024,256]{1,0:T(8,128)(2,1)S(1)}, bf16[256,1024]{1,0:T(8,128)(2,1)S(1)}) custom-call(bf16[2,128,256]{2,1,0:T(8,128)(2,1)S(1)} %get-tuple-element.14.refs_0_, f32[2,128,256]{2,1,0:T(8,128)S(1)} %get-tuple-element.13.refs_1_.refs_0_, bf16[1,128,256]{2,1,0:T(8,128)(2,1)S(1)} %get-tuple-element.30.refs_2_, ...), custom_call_target="tpu_custom_call" | custom-call | tf_op jit(solution)/shard_map/square_step/pallas_call | solution.py:165
  18.5 1.8 %collective-permute-start.8 = (bf16[1,2,128,256]{3,2,1,0:T(8,128)(2,1)S(1)}, bf16[1,2,128,256]{3,2,1,0:T(8,128)(2,1)S(1)}, u32[]{:S(2)}, u32[]{:S(2)}) collective-permute-start(bf16[1,2,128,256]{3,2,1,0:T(8,128)(2,1)S(1)} %bitcast.30), channel_id=1, source_target_pairs={{0,2},{1,3},{2,0},{3,1},{4,6},{5,7},{6,4},{7,5},{8,10},{9,11},{10,... | collective-permute-start | bytes 393224 | tf_op jit(solution)/shard_map/ppermute | solution.py:87
  20.3 1.9 %collective-permute-start.7 = (bf16[1,2,128,256]{3,2,1,0:T(8,128)(2,1)S(1)}, bf16[1,2,128,256]{3,2,1,0:T(8,128)(2,1)S(1)}, u32[]{:S(2)}, u32[]{:S(2)}) collective-permute-start(bf16[1,2,128,256]{3,2,1,0:T(8,128)(2,1)S(1)} %bitcast.31), channel_id=1, source_target_pairs={{0,1},{1,0},{2,3},{3,2},{4,5},{5,4},{6,7},{7,6},{8,9},{9,8},{10,11... | collective-permute-start | bytes 393224 | tf_op jit(solution)/shard_map/ppermute | solution.py:87
  22.2 1.3 %collective-permute-start.10 = (bf16[1,128,256]{2,1,0:T(8,128)(2,1)S(1)}, bf16[1,128,256]{2,1,0:T(8,128)(2,1)S(1)}, u32[]{:S(2)}, u32[]{:S(2)}) collective-permute-start(bf16[1,128,256]{2,1,0:T(8,128)(2,1)S(1)} %get-tuple-element.32.refs_5_), channel_id=1, source_target_pairs={{0,8},{4,12},{8,0},{12,4},{16,24},{20,28},{24,16},{28,20},{1,9},{5... | collective-permute-start | bytes 196616 | tf_op jit(solution)/shard_map/ppermute | solution.py:87
  23.6 1.6 %collective-permute-start.11 = (bf16[1,2,128,256]{3,2,1,0:T(8,128)(2,1)S(1)}, bf16[1,2,128,256]{3,2,1,0:T(8,128)(2,1)S(1)}, u32[]{:S(2)}, u32[]{:S(2)}) collective-permute-start(bf16[1,2,128,256]{3,2,1,0:T(8,128)(2,1)S(1)} %pad_maximum_fusion.1), channel_id=1, source_target_pairs={{0,16},{4,20},{8,24},{12,28},{16,0},{20,4},{24,8},{28,12},{1,17},{... | collective-permute-start | bytes 393224 | tf_op jit(solution)/shard_map/ppermute | solution.py:87
  25.2 1.3 %collective-permute-done.10.refs_6_ = bf16[1,128,256]{2,1,0:T(8,128)(2,1)S(1)} collective-permute-done((bf16[1,128,256]{2,1,0:T(8,128)(2,1)S(1)}, bf16[1,128,256]{2,1,0:T(8,128)(2,1)S(1)}, u32[]{:S(2)}, u32[]{:S(2)}) %collective-permute-start.10) | collective-permute-done | bytes 65568 | tf_op jit(solution)/shard_map/ppermute | solution.py:87
  26.5 1.6 %collective-permute-start.13 = (bf16[1,2,128,256]{3,2,1,0:T(8,128)(2,1)S(1)}, bf16[1,2,128,256]{3,2,1,0:T(8,128)(2,1)S(1)}, u32[]{:S(2)}, u32[]{:S(2)}) collective-permute-start(bf16[1,2,128,256]{3,2,1,0:T(8,128)(2,1)S(1)} %pad_maximum_fusion.2), channel_id=1, source_target_pairs={{0,16},{4,20},{8,24},{12,28},{16,0},{20,4},{24,8},{28,12},{1,17},{... | collective-permute-start | bytes 393224 | tf_op jit(solution)/shard_map/ppermute | solution.py:87
  28.2 1.6 %collective-permute-done.11 = bf16[1,2,128,256]{3,2,1,0:T(8,128)(2,1)S(1)} collective-permute-done((bf16[1,2,128,256]{3,2,1,0:T(8,128)(2,1)S(1)}, bf16[1,2,128,256]{3,2,1,0:T(8,128)(2,1)S(1)}, u32[]{:S(2)}, u32[]{:S(2)}) %collective-permute-start.11) | collective-permute-done | bytes 131104 | tf_op jit(solution)/shard_map/ppermute | solution.py:87
  29.8 1.7 %collective-permute-done.13 = bf16[1,2,128,256]{3,2,1,0:T(8,128)(2,1)S(1)} collective-permute-done((bf16[1,2,128,256]{3,2,1,0:T(8,128)(2,1)S(1)}, bf16[1,2,128,256]{3,2,1,0:T(8,128)(2,1)S(1)}, u32[]{:S(2)}, u32[]{:S(2)}) %collective-permute-start.13) | collective-permute-done | bytes 131104 | tf_op jit(solution)/shard_map/ppermute | solution.py:87
  31.8 1.3 %collective-permute-done.9.refs_6_ = bf16[1,2,128,256]{3,2,1,0:T(8,128)(2,1)S(1)} collective-permute-done((bf16[1,2,128,256]{3,2,1,0:T(8,128)(2,1)S(1)}, bf16[1,2,128,256]{3,2,1,0:T(8,128)(2,1)S(1)}, u32[]{:S(2)}, u32[]{:S(2)}) %collective-permute-start.9) | collective-permute-done | bytes 131104 | tf_op jit(solution)/shard_map/ppermute | solution.py:87
  33.1 0.4 %purify_step.1 = (bf16[128,256]{1,0:T(8,128)(2,1)S(1)}, f32[128,256]{1,0:T(8,128)S(1)}, bf16[128,1024]{1,0:T(8,128)(2,1)S(1)}) custom-call(bf16[2,128,256]{2,1,0:T(8,128)(2,1)S(1)} %get-tuple-element.15.refs_0_, f32[2,128,256]{2,1,0:T(8,128)S(1)} %get-tuple-element.13.refs_1_.refs_0_, bf16[1024,256]{1,0:T(8,128)(2,1)S(1)} %get-tuple-element.16.refs_2_, ...), custom_call_target="tpu_custom_call" | custom-call | flops 6000000000 | tf_op jit(solution)/shard_map/purify_step/pallas_call | solution.py:165
  33.4 0.2 collective-permute-done.14.refs_9_
  33.7 1.0 %last_step.1 = (bf16[128,256]{1,0:T(8,128)(2,1)}, bf16[128,256]{1,0:T(8,128)(2,1)}) custom-call(f32[2,128,256]{2,1,0:T(8,128)S(1)} %get-tuple-element.13.refs_1_.refs_0_, bf16[128,256]{1,0:T(8,128)(2,1)S(1)} %get-tuple-element.19.refs_1_, f32[128,256]{1,0:T(8,128)S(1)} %get-tuple-element.20.refs_2_, bf16[256,1024]{1,0:T(8,128)(2,1)S(1)} %get-tuple-element.21.refs_3_, ...), custom_call_target="tpu_custom_call" | custom-call | tf_op jit(solution)/shard_map/last_step/pallas_call | solution.py:165
  (21 shorter events, 0.6 us)
Async XLA Ops:
  1.6 11.5 %collective-permute-start.4 = (bf16[1,2,128,256]{3,2,1,0:T(8,128)(2,1)S(1)}, bf16[1,2,128,256]{3,2,1,0:T(8,128)(2,1)S(1)}, u32[]{:S(2)}, u32[]{:S(2)}) collective-permute-start(bf16[1,2,128,256]{3,2,1,0:T(8,128)(2,1)S(1)} %bitcast.24), channel_id=1, source_target_pairs={{0,2},{1,3},{2,0},{3,1},{4,6},{5,7},{6,4},{7,5},{8,10},{9,11},{10,... | collective-permute-start | bytes 393224 | tf_op jit(solution)/shard_map/ppermute | solution.py:87
  5.7 4.3 %collective-permute-start = (bf16[1,128,256]{2,1,0:T(8,128)(2,1)S(1)}, bf16[1,128,256]{2,1,0:T(8,128)(2,1)S(1)}, u32[]{:S(2)}, u32[]{:S(2)}) collective-permute-start(bf16[1,128,256]{2,1,0:T(8,128)(2,1)S(1)} %get-tuple-element.30.refs_2_), channel_id=1, source_target_pairs={{0,16},{4,20},{8,24},{12,28},{16,0},{20,4},{24,8},{28,12},{1,17},{... | collective-permute-start | bytes 196616 | tf_op jit(solution)/shard_map/ppermute | solution.py:87
  7.3 7.0 %collective-permute-start.1 = (bf16[1,128,256]{2,1,0:T(8,128)(2,1)S(1)}, bf16[1,128,256]{2,1,0:T(8,128)(2,1)S(1)}, u32[]{:S(2)}, u32[]{:S(2)}) collective-permute-start(bf16[1,128,256]{2,1,0:T(8,128)(2,1)S(1)} %get-tuple-element.30.refs_2_), channel_id=1, source_target_pairs={{0,8},{4,12},{8,0},{12,4},{16,24},{20,28},{24,16},{28,20},{1,9},{5... | collective-permute-start | bytes 196616 | tf_op jit(solution)/shard_map/ppermute | solution.py:87
  10.0 4.3 %collective-permute-start.2 = (bf16[1,128,256]{2,1,0:T(8,128)(2,1)S(1)}, bf16[1,128,256]{2,1,0:T(8,128)(2,1)S(1)}, u32[]{:S(2)}, u32[]{:S(2)}) collective-permute-start(bf16[1,128,256]{2,1,0:T(8,128)(2,1)S(1)} %collective-permute-done.refs_3_), channel_id=1, source_target_pairs={{0,8},{4,12},{8,0},{12,4},{16,24},{20,28},{24,16},{28,20},{1,9},{5... | collective-permute-start | bytes 196616 | tf_op jit(solution)/shard_map/ppermute | solution.py:87
  11.5 5.1 %collective-permute-start.5 = (bf16[1,2,128,256]{3,2,1,0:T(8,128)(2,1)S(1)}, bf16[1,2,128,256]{3,2,1,0:T(8,128)(2,1)S(1)}, u32[]{:S(2)}, u32[]{:S(2)}) collective-permute-start(bf16[1,2,128,256]{3,2,1,0:T(8,128)(2,1)S(1)} %bitcast.26), channel_id=1, source_target_pairs={{0,1},{1,0},{2,3},{3,2},{4,5},{5,4},{6,7},{7,6},{8,9},{9,8},{10,11... | collective-permute-start | bytes 393224 | tf_op jit(solution)/shard_map/ppermute | solution.py:87
  13.1 5.0 %collective-permute-start.6 = (bf16[1,2,128,256]{3,2,1,0:T(8,128)(2,1)S(1)}, bf16[1,2,128,256]{3,2,1,0:T(8,128)(2,1)S(1)}, u32[]{:S(2)}, u32[]{:S(2)}) collective-permute-start(bf16[1,2,128,256]{3,2,1,0:T(8,128)(2,1)S(1)} %collective-permute-done.4.refs_8_), channel_id=1, source_target_pairs={{0,1},{1,0},{2,3},{3,2},{4,5},{5,4},{6,7},{7,6},{8,9},{9,8},{10,11... | collective-permute-start | bytes 393224 | tf_op jit(solution)/shard_map/ppermute | solution.py:87
  13.6 11.6 %collective-permute-start.12 = (bf16[1,128,256]{2,1,0:T(8,128)(2,1)S(1)}, bf16[1,128,256]{2,1,0:T(8,128)(2,1)S(1)}, u32[]{:S(2)}, u32[]{:S(2)}) collective-permute-start(bf16[1,128,256]{2,1,0:T(8,128)(2,1)S(1)} %get-tuple-element.23.refs_10_), channel_id=1, source_target_pairs={{0,8},{4,12},{8,0},{12,4},{16,24},{20,28},{24,16},{28,20},{1,9},{5... | collective-permute-start | bytes 196616 | tf_op jit(solution)/shard_map/ppermute | solution.py:87
  14.3 3.8 %collective-permute-start.3 = (bf16[1,4,128,256]{3,2,1,0:T(8,128)(2,1)S(1)}, bf16[1,4,128,256]{3,2,1,0:T(8,128)(2,1)S(1)}, u32[]{:S(2)}, u32[]{:S(2)}) collective-permute-start(bf16[1,4,128,256]{3,2,1,0:T(8,128)(2,1)S(1)} %maximum_bitcast_fusion), channel_id=1, source_target_pairs={{0,4},{4,0},{8,12},{12,8},{16,20},{20,16},{24,28},{28,24},{1,5},{5... | collective-permute-start | bytes 786440 | tf_op jit(solution)/shard_map/ppermute | solution.py:268
  18.5 9.6 %collective-permute-start.8 = (bf16[1,2,128,256]{3,2,1,0:T(8,128)(2,1)S(1)}, bf16[1,2,128,256]{3,2,1,0:T(8,128)(2,1)S(1)}, u32[]{:S(2)}, u32[]{:S(2)}) collective-permute-start(bf16[1,2,128,256]{3,2,1,0:T(8,128)(2,1)S(1)} %bitcast.30), channel_id=1, source_target_pairs={{0,2},{1,3},{2,0},{3,1},{4,6},{5,7},{6,4},{7,5},{8,10},{9,11},{10,... | collective-permute-start | bytes 393224 | tf_op jit(solution)/shard_map/ppermute | solution.py:87
  20.3 7.8 %collective-permute-start.7 = (bf16[1,2,128,256]{3,2,1,0:T(8,128)(2,1)S(1)}, bf16[1,2,128,256]{3,2,1,0:T(8,128)(2,1)S(1)}, u32[]{:S(2)}, u32[]{:S(2)}) collective-permute-start(bf16[1,2,128,256]{3,2,1,0:T(8,128)(2,1)S(1)} %bitcast.31), channel_id=1, source_target_pairs={{0,1},{1,0},{2,3},{3,2},{4,5},{5,4},{6,7},{7,6},{8,9},{9,8},{10,11... | collective-permute-start | bytes 393224 | tf_op jit(solution)/shard_map/ppermute | solution.py:87
  22.2 4.3 %collective-permute-start.10 = (bf16[1,128,256]{2,1,0:T(8,128)(2,1)S(1)}, bf16[1,128,256]{2,1,0:T(8,128)(2,1)S(1)}, u32[]{:S(2)}, u32[]{:S(2)}) collective-permute-start(bf16[1,128,256]{2,1,0:T(8,128)(2,1)S(1)} %get-tuple-element.32.refs_5_), channel_id=1, source_target_pairs={{0,8},{4,12},{8,0},{12,4},{16,24},{20,28},{24,16},{28,20},{1,9},{5... | collective-permute-start | bytes 196616 | tf_op jit(solution)/shard_map/ppermute | solution.py:87
  23.6 6.2 %collective-permute-start.11 = (bf16[1,2,128,256]{3,2,1,0:T(8,128)(2,1)S(1)}, bf16[1,2,128,256]{3,2,1,0:T(8,128)(2,1)S(1)}, u32[]{:S(2)}, u32[]{:S(2)}) collective-permute-start(bf16[1,2,128,256]{3,2,1,0:T(8,128)(2,1)S(1)} %pad_maximum_fusion.1), channel_id=1, source_target_pairs={{0,16},{4,20},{8,24},{12,28},{16,0},{20,4},{24,8},{28,12},{1,17},{... | collective-permute-start | bytes 393224 | tf_op jit(solution)/shard_map/ppermute | solution.py:87
  26.5 5.0 %collective-permute-start.13 = (bf16[1,2,128,256]{3,2,1,0:T(8,128)(2,1)S(1)}, bf16[1,2,128,256]{3,2,1,0:T(8,128)(2,1)S(1)}, u32[]{:S(2)}, u32[]{:S(2)}) collective-permute-start(bf16[1,2,128,256]{3,2,1,0:T(8,128)(2,1)S(1)} %pad_maximum_fusion.2), channel_id=1, source_target_pairs={{0,16},{4,20},{8,24},{12,28},{16,0},{20,4},{24,8},{28,12},{1,17},{... | collective-permute-start | bytes 393224 | tf_op jit(solution)/shard_map/ppermute | solution.py:87
  28.1 5.0 %collective-permute-start.9 = (bf16[1,2,128,256]{3,2,1,0:T(8,128)(2,1)S(1)}, bf16[1,2,128,256]{3,2,1,0:T(8,128)(2,1)S(1)}, u32[]{:S(2)}, u32[]{:S(2)}) collective-permute-start(bf16[1,2,128,256]{3,2,1,0:T(8,128)(2,1)S(1)} %collective-permute-done.8.refs_4_), channel_id=1, source_target_pairs={{0,1},{1,0},{2,3},{3,2},{4,5},{5,4},{6,7},{7,6},{8,9},{9,8},{10,11... | collective-permute-start | bytes 393224 | tf_op jit(solution)/shard_map/ppermute | solution.py:87
  31.7 2.0 %collective-permute-start.14 = (bf16[2,4,128,256]{3,2,1,0:T(8,128)(2,1)S(1)}, bf16[2,4,128,256]{3,2,1,0:T(8,128)(2,1)S(1)}, u32[]{:S(2)}, u32[]{:S(2)}) collective-permute-start(bf16[2,4,128,256]{3,2,1,0:T(8,128)(2,1)S(1)} %pad_maximum_fusion), channel_id=1, source_target_pairs={{0,4},{4,0},{8,12},{12,8},{16,20},{20,16},{24,28},{28,24},{1,5},{5... | collective-permute-start | bytes 1572872 | tf_op jit(solution)/shard_map/ppermute | solution.py:268

commit v4 on v3

--- a/solution.py
+++ b/solution.py
@@ -7,7 +7,6 @@
 
 IN_HBM = pl.BlockSpec(memory_space=pltpu.HBM)
 IN_VMEM = pl.BlockSpec(memory_space=pltpu.VMEM)
-SOON = pl.CostEstimate(flops=100_000_000, bytes_accessed=0, transcendentals=0)
 LIMIT = pltpu.CompilerParams(vmem_limit_bytes=32 * 1024 * 1024)
 EARLY = pl.CostEstimate(flops=6_000_000_000, bytes_accessed=0, transcendentals=0)
 
@@ -116,10 +115,7 @@
     far = swap(held, axis_name, size, flips[-2:-1])
     near = swap(held, axis_name, size, flips[-1:])
     _, later = tie([far, later])
-    if settled:
-        near = [(ats, settle(pairs, SOON)) for ats, pairs in near]
-    else:
-        near, far = tie([near, far])
+    near, far = tie([near, far])
     last = swap(far, axis_name, size, flips[-1:])
     if settled:
         last = [(ats, settle(pairs, EARLY)) for ats, pairs in last]
@@ -280,9 +276,7 @@
     own = double([([0], pair[None])], "row", n_row, lead)
     masked, filtered = cut(own, 0), cut(own, 1)
     pair_held, later = exchange(pair, "col", n_col, True, filtered)
-    far = swap(masked, "row", n_row, first)
-    near = swap(masked, "row", n_row, second)
-    masked = masked + far + near + swap(far, "row", n_row, second)
+    masked = double(masked, "row", n_row, first + second)
     other = swap(later, "row", n_row, second)
     (masked_blocks,) = across_cores([masked], n_row)
     both, masked_cols, pair_rows = square_step(pair, kept, masked_blocks, pair_held)

time: 34.8 us -> 35.9 us (1.032)
  waiting for transfers between devices: 11.1 us -> 12.4 us
    ppermute x2, waiting for transfers between devices: 0.23 us -> 0.98 us  [across_cores(): lax.ppermute(sent, 'row', [(i, i ^ flip) for i in range(n_row)])]
    ppermute x13 -> x12, waiting for transfers between devices: 10.9 us -> 11.5 us  [swap(): lax.ppermute(blocks, axis_name, [(i, i ^ flip) for i in range(size)])]
    ppermute x13 -> x12, starting transfers between devices: 19.7 us -> 19.5 us  [swap(): lax.ppermute(blocks, axis_name, [(i, i ^ flip) for i in range(size)])]
  transfers between devices with their start and end apart: 15 -> 14, of which waited for: 8 -> 9; matrix products, arithmetic and copies ran while one was open for 1% -> 1% of each run, Pallas kernels for 2% -> 2%
where the time goes in v4:
time: 35.9 us; the launch traced here: 35.8 us
  starting transfers between devices  19.6 us (55%)
  waiting for transfers between devices  12.4 us (35%)
  Pallas kernels  2.73 us (8%)
  between operations  0.75 us (2%)
    ppermute x12, starting transfers between devices, swap(): lax.ppermute(blocks, axis_name, [(i, i ^ flip) for i in range(size)])  19.5 us
    ppermute x12, waiting for transfers between devices, swap(): lax.ppermute(blocks, axis_name, [(i, i ^ flip) for i in range(size)])  11.5 us
    pallas_call x3, Pallas kernels, call(): pl.pallas_call(body, out_shape=out_shape, in_specs=[IN_VMEM] * len(arrays...  1.78 us
    ppermute x2, waiting for transfers between devices, across_cores(): lax.ppermute(sent, 'row', [(i, i ^ flip) for i in range(n_row)])  0.98 us
    pallas_call x1, Pallas kernels, mask(): pl.pallas_call(kernel, out_shape=(pltpu.VMEM((2, height, width), density....  0.94 us
  transfers between devices with their start and end apart: 14, of which 9 were waited for; matrix products, arithmetic and copies ran while one was open for 1% of the time, Pallas kernels for 2%

profile of v4, /device:TPU:0, one launch (start us, length us, event | category | flops | bytes accessed | tf_op | source)
XLA Modules:
  0.0 35.8 jit_solution(3420319789311857516)
XLA Ops:
  0.6 0.9 %mask.1 = (bf16[2,128,256]{2,1,0:T(8,128)(2,1)S(1)}, f32[2,128,256]{2,1,0:T(8,128)S(1)}) custom-call(s32[2,4]{1,0:T(2,128)} %refs_0_.1, s32[2,4]{1,0:T(2,128)} %refs_1_.1, bf16[128,256]{1,0:T(8,128)(2,1)} %refs_2_.1, bf16[128,256]{1,0:T(8,128)(2,1)} %refs_3_.1), custom_call_target="tpu_custom_call" | custom-call | tf_op jit(solution)/shard_map/mask/pallas_call | solution.py:44
  1.6 3.0 %collective-permute-start = (bf16[1,128,256]{2,1,0:T(8,128)(2,1)S(1)}, bf16[1,128,256]{2,1,0:T(8,128)(2,1)S(1)}, u32[]{:S(2)}, u32[]{:S(2)}) collective-permute-start(bf16[1,128,256]{2,1,0:T(8,128)(2,1)S(1)} %get-tuple-element.34.refs_2_), channel_id=1, source_target_pairs={{0,16},{4,20},{8,24},{12,28},{16,0},{20,4},{24,8},{28,12},{1,17},{... | collective-permute-start | bytes 196616 | tf_op jit(solution)/shard_map/ppermute | solution.py:86
  4.6 2.6 %collective-permute-start.4 = (bf16[1,2,128,256]{3,2,1,0:T(8,128)(2,1)S(1)}, bf16[1,2,128,256]{3,2,1,0:T(8,128)(2,1)S(1)}, u32[]{:S(2)}, u32[]{:S(2)}) collective-permute-start(bf16[1,2,128,256]{3,2,1,0:T(8,128)(2,1)S(1)} %bitcast.25), channel_id=1, source_target_pairs={{0,2},{1,3},{2,0},{3,1},{4,6},{5,7},{6,4},{7,5},{8,10},{9,11},{10,... | collective-permute-start | bytes 393224 | tf_op jit(solution)/shard_map/ppermute | solution.py:86
  7.2 1.6 %collective-permute-start.3 = (bf16[1,2,128,256]{3,2,1,0:T(8,128)(2,1)S(1)}, bf16[1,2,128,256]{3,2,1,0:T(8,128)(2,1)S(1)}, u32[]{:S(2)}, u32[]{:S(2)}) collective-permute-start(bf16[1,2,128,256]{3,2,1,0:T(8,128)(2,1)S(1)} %bitcast.26), channel_id=1, source_target_pairs={{0,1},{1,0},{2,3},{3,2},{4,5},{5,4},{6,7},{7,6},{8,9},{9,8},{10,11... | collective-permute-start | bytes 393224 | tf_op jit(solution)/shard_map/ppermute | solution.py:86
  8.8 1.6 %collective-permute-start.1 = (bf16[2,128,256]{2,1,0:T(8,128)(2,1)S(1)}, bf16[2,128,256]{2,1,0:T(8,128)(2,1)S(1)}, u32[]{:S(2)}, u32[]{:S(2)}) collective-permute-start(bf16[2,128,256]{2,1,0:T(8,128)(2,1)S(1)} %pad_maximum_fusion.1), channel_id=1, source_target_pairs={{0,8},{4,12},{8,0},{12,4},{16,24},{20,28},{24,16},{28,20},{1,9},{5... | collective-permute-start | bytes 393224 | tf_op jit(solution)/shard_map/ppermute | solution.py:86
  10.4 3.0 %collective-permute-done.4.refs_7_ = bf16[1,2,128,256]{3,2,1,0:T(8,128)(2,1)S(1)} collective-permute-done((bf16[1,2,128,256]{3,2,1,0:T(8,128)(2,1)S(1)}, bf16[1,2,128,256]{3,2,1,0:T(8,128)(2,1)S(1)}, u32[]{:S(2)}, u32[]{:S(2)}) %collective-permute-start.4) | collective-permute-done | bytes 131104 | tf_op jit(solution)/shard_map/ppermute | solution.py:86
  13.6 1.4 %collective-permute-start.5 = (bf16[1,2,128,256]{3,2,1,0:T(8,128)(2,1)S(1)}, bf16[1,2,128,256]{3,2,1,0:T(8,128)(2,1)S(1)}, u32[]{:S(2)}, u32[]{:S(2)}) collective-permute-start(bf16[1,2,128,256]{3,2,1,0:T(8,128)(2,1)S(1)} %collective-permute-done.4.refs_7_), channel_id=1, source_target_pairs={{0,1},{1,0},{2,3},{3,2},{4,5},{5,4},{6,7},{7,6},{8,9},{9,8},{10,11... | collective-permute-start | bytes 393224 | tf_op jit(solution)/shard_map/ppermute | solution.py:86
  15.0 1.5 %collective-permute-start.11 = (bf16[1,128,256]{2,1,0:T(8,128)(2,1)S(1)}, bf16[1,128,256]{2,1,0:T(8,128)(2,1)S(1)}, u32[]{:S(2)}, u32[]{:S(2)}) collective-permute-start(bf16[1,128,256]{2,1,0:T(8,128)(2,1)S(1)} %get-tuple-element.27.refs_10_), channel_id=1, source_target_pairs={{0,8},{4,12},{8,0},{12,4},{16,24},{20,28},{24,16},{28,20},{1,9},{5... | collective-permute-start | bytes 196616 | tf_op jit(solution)/shard_map/ppermute | solution.py:86
  16.6 2.0 %collective-permute-done.5.block_ref = bf16[1,2,128,256]{3,2,1,0:T(8,128)(2,1)S(1)} collective-permute-done((bf16[1,2,128,256]{3,2,1,0:T(8,128)(2,1)S(1)}, bf16[1,2,128,256]{3,2,1,0:T(8,128)(2,1)S(1)}, u32[]{:S(2)}, u32[]{:S(2)}) %collective-permute-start.5) | collective-permute-done | bytes 131104 | tf_op jit(solution)/shard_map/ppermute | solution.py:86
  18.6 0.4 %square_step.1 = (bf16[2,128,256]{2,1,0:T(8,128)(2,1)S(1)}, bf16[1024,256]{1,0:T(8,128)(2,1)S(1)}, bf16[256,1024]{1,0:T(8,128)(2,1)S(1)}) custom-call(bf16[2,128,256]{2,1,0:T(8,128)(2,1)S(1)} %get-tuple-element.16.refs_0_, f32[2,128,256]{2,1,0:T(8,128)S(1)} %get-tuple-element.15.refs_1_.refs_0_, bf16[1,128,256]{2,1,0:T(8,128)(2,1)S(1)} %get-tuple-element.34.refs_2_, ...), custom_call_target="tpu_custom_call" | custom-call | tf_op jit(solution)/shard_map/square_step/pallas_call | solution.py:161
  19.0 2.5 %collective-permute-start.7 = (bf16[1,2,128,256]{3,2,1,0:T(8,128)(2,1)S(1)}, bf16[1,2,128,256]{3,2,1,0:T(8,128)(2,1)S(1)}, u32[]{:S(2)}, u32[]{:S(2)}) collective-permute-start(bf16[1,2,128,256]{3,2,1,0:T(8,128)(2,1)S(1)} %bitcast.30), channel_id=1, source_target_pairs={{0,2},{1,3},{2,0},{3,1},{4,6},{5,7},{6,4},{7,5},{8,10},{9,11},{10,... | collective-permute-start | bytes 393224 | tf_op jit(solution)/shard_map/ppermute | solution.py:86
  21.5 1.7 %collective-permute-start.6 = (bf16[1,2,128,256]{3,2,1,0:T(8,128)(2,1)S(1)}, bf16[1,2,128,256]{3,2,1,0:T(8,128)(2,1)S(1)}, u32[]{:S(2)}, u32[]{:S(2)}) collective-permute-start(bf16[1,2,128,256]{3,2,1,0:T(8,128)(2,1)S(1)} %bitcast.31), channel_id=1, source_target_pairs={{0,1},{1,0},{2,3},{3,2},{4,5},{5,4},{6,7},{7,6},{8,9},{9,8},{10,11... | collective-permute-start | bytes 393224 | tf_op jit(solution)/shard_map/ppermute | solution.py:86
  23.3 1.5 %collective-permute-start.9 = (bf16[1,128,256]{2,1,0:T(8,128)(2,1)S(1)}, bf16[1,128,256]{2,1,0:T(8,128)(2,1)S(1)}, u32[]{:S(2)}, u32[]{:S(2)}) collective-permute-start(bf16[1,128,256]{2,1,0:T(8,128)(2,1)S(1)} %get-tuple-element.36.refs_5_), channel_id=1, source_target_pairs={{0,8},{4,12},{8,0},{12,4},{16,24},{20,28},{24,16},{28,20},{1,9},{5... | collective-permute-start | bytes 196616 | tf_op jit(solution)/shard_map/ppermute | solution.py:86
  24.8 0.6 %collective-permute-start.10 = (bf16[1,2,128,256]{3,2,1,0:T(8,128)(2,1)S(1)}, bf16[1,2,128,256]{3,2,1,0:T(8,128)(2,1)S(1)}, u32[]{:S(2)}, u32[]{:S(2)}) collective-permute-start(bf16[1,2,128,256]{3,2,1,0:T(8,128)(2,1)S(1)} %pad_maximum_fusion.2), channel_id=1, source_target_pairs={{0,16},{4,20},{8,24},{12,28},{16,0},{20,4},{24,8},{28,12},{1,17},{... | collective-permute-start | bytes 393224 | tf_op jit(solution)/shard_map/ppermute | solution.py:86
  25.4 2.2 %collective-permute-done.9.refs_6_ = bf16[1,128,256]{2,1,0:T(8,128)(2,1)S(1)} collective-permute-done((bf16[1,128,256]{2,1,0:T(8,128)(2,1)S(1)}, bf16[1,128,256]{2,1,0:T(8,128)(2,1)S(1)}, u32[]{:S(2)}, u32[]{:S(2)}) %collective-permute-start.9) | collective-permute-done | bytes 65568 | tf_op jit(solution)/shard_map/ppermute | solution.py:86
  27.6 0.6 %collective-permute-start.12 = (bf16[1,2,128,256]{3,2,1,0:T(8,128)(2,1)S(1)}, bf16[1,2,128,256]{3,2,1,0:T(8,128)(2,1)S(1)}, u32[]{:S(2)}, u32[]{:S(2)}) collective-permute-start(bf16[1,2,128,256]{3,2,1,0:T(8,128)(2,1)S(1)} %pad_maximum_fusion.3), channel_id=1, source_target_pairs={{0,16},{4,20},{8,24},{12,28},{16,0},{20,4},{24,8},{28,12},{1,17},{... | collective-permute-start | bytes 393224 | tf_op jit(solution)/shard_map/ppermute | solution.py:86
  28.1 0.3 collective-permute-done.6.refs_5_
  28.4 0.9 %collective-permute-start.8 = (bf16[1,2,128,256]{3,2,1,0:T(8,128)(2,1)S(1)}, bf16[1,2,128,256]{3,2,1,0:T(8,128)(2,1)S(1)}, u32[]{:S(2)}, u32[]{:S(2)}) collective-permute-start(bf16[1,2,128,256]{3,2,1,0:T(8,128)(2,1)S(1)} %collective-permute-done.7.refs_4_), channel_id=1, source_target_pairs={{0,1},{1,0},{2,3},{3,2},{4,5},{5,4},{6,7},{7,6},{8,9},{9,8},{10,11... | collective-permute-start | bytes 393224 | tf_op jit(solution)/shard_map/ppermute | solution.py:86
  29.4 1.4 %collective-permute-done.10 = bf16[1,2,128,256]{3,2,1,0:T(8,128)(2,1)S(1)} collective-permute-done((bf16[1,2,128,256]{3,2,1,0:T(8,128)(2,1)S(1)}, bf16[1,2,128,256]{3,2,1,0:T(8,128)(2,1)S(1)}, u32[]{:S(2)}, u32[]{:S(2)}) %collective-permute-start.10) | collective-permute-done | bytes 131104 | tf_op jit(solution)/shard_map/ppermute | solution.py:86
  30.8 1.8 %collective-permute-done.12 = bf16[1,2,128,256]{3,2,1,0:T(8,128)(2,1)S(1)} collective-permute-done((bf16[1,2,128,256]{3,2,1,0:T(8,128)(2,1)S(1)}, bf16[1,2,128,256]{3,2,1,0:T(8,128)(2,1)S(1)}, u32[]{:S(2)}, u32[]{:S(2)}) %collective-permute-start.12) | collective-permute-done | bytes 131104 | tf_op jit(solution)/shard_map/ppermute | solution.py:86
  32.8 0.6 %collective-permute-done.8.refs_6_ = bf16[1,2,128,256]{3,2,1,0:T(8,128)(2,1)S(1)} collective-permute-done((bf16[1,2,128,256]{3,2,1,0:T(8,128)(2,1)S(1)}, bf16[1,2,128,256]{3,2,1,0:T(8,128)(2,1)S(1)}, u32[]{:S(2)}, u32[]{:S(2)}) %collective-permute-start.8) | collective-permute-done | bytes 131104 | tf_op jit(solution)/shard_map/ppermute | solution.py:86
  33.4 0.4 %purify_step.1 = (bf16[128,256]{1,0:T(8,128)(2,1)S(1)}, f32[128,256]{1,0:T(8,128)S(1)}, bf16[128,1024]{1,0:T(8,128)(2,1)S(1)}) custom-call(bf16[2,128,256]{2,1,0:T(8,128)(2,1)S(1)} %get-tuple-element.19.refs_0_, f32[2,128,256]{2,1,0:T(8,128)S(1)} %get-tuple-element.15.refs_1_.refs_0_, bf16[1024,256]{1,0:T(8,128)(2,1)S(1)} %get-tuple-element.20.refs_2_, ...), custom_call_target="tpu_custom_call" | custom-call | flops 6000000000 | tf_op jit(solution)/shard_map/purify_step/pallas_call | solution.py:161
  33.8 1.0 %collective-permute-done.13.refs_9_ = bf16[2,4,128,256]{3,2,1,0:T(8,128)(2,1)S(1)} collective-permute-done((bf16[2,4,128,256]{3,2,1,0:T(8,128)(2,1)S(1)}, bf16[2,4,128,256]{3,2,1,0:T(8,128)(2,1)S(1)}, u32[]{:S(2)}, u32[]{:S(2)}) %collective-permute-start.13) | collective-permute-done | bytes 524320 | tf_op jit(solution)/shard_map/ppermute | solution.py:264
  34.7 1.0 %last_step.1 = (bf16[128,256]{1,0:T(8,128)(2,1)}, bf16[128,256]{1,0:T(8,128)(2,1)}) custom-call(f32[2,128,256]{2,1,0:T(8,128)S(1)} %get-tuple-element.15.refs_1_.refs_0_, bf16[128,256]{1,0:T(8,128)(2,1)S(1)} %get-tuple-element.23.refs_1_, f32[128,256]{1,0:T(8,128)S(1)} %get-tuple-element.24.refs_2_, bf16[256,1024]{1,0:T(8,128)(2,1)S(1)} %get-tuple-element.25.refs_3_, ...), custom_call_target="tpu_custom_call" | custom-call | tf_op jit(solution)/shard_map/last_step/pallas_call | solution.py:161
  (19 shorter events, 0.6 us)
Async XLA Ops:
  1.6 7.2 %collective-permute-start = (bf16[1,128,256]{2,1,0:T(8,128)(2,1)S(1)}, bf16[1,128,256]{2,1,0:T(8,128)(2,1)S(1)}, u32[]{:S(2)}, u32[]{:S(2)}) collective-permute-start(bf16[1,128,256]{2,1,0:T(8,128)(2,1)S(1)} %get-tuple-element.34.refs_2_), channel_id=1, source_target_pairs={{0,16},{4,20},{8,24},{12,28},{16,0},{20,4},{24,8},{28,12},{1,17},{... | collective-permute-start | bytes 196616 | tf_op jit(solution)/shard_map/ppermute | solution.py:86
  4.6 8.8 %collective-permute-start.4 = (bf16[1,2,128,256]{3,2,1,0:T(8,128)(2,1)S(1)}, bf16[1,2,128,256]{3,2,1,0:T(8,128)(2,1)S(1)}, u32[]{:S(2)}, u32[]{:S(2)}) collective-permute-start(bf16[1,2,128,256]{3,2,1,0:T(8,128)(2,1)S(1)} %bitcast.25), channel_id=1, source_target_pairs={{0,2},{1,3},{2,0},{3,1},{4,6},{5,7},{6,4},{7,5},{8,10},{9,11},{10,... | collective-permute-start | bytes 393224 | tf_op jit(solution)/shard_map/ppermute | solution.py:86
  7.2 6.4 %collective-permute-start.3 = (bf16[1,2,128,256]{3,2,1,0:T(8,128)(2,1)S(1)}, bf16[1,2,128,256]{3,2,1,0:T(8,128)(2,1)S(1)}, u32[]{:S(2)}, u32[]{:S(2)}) collective-permute-start(bf16[1,2,128,256]{3,2,1,0:T(8,128)(2,1)S(1)} %bitcast.26), channel_id=1, source_target_pairs={{0,1},{1,0},{2,3},{3,2},{4,5},{5,4},{6,7},{7,6},{8,9},{9,8},{10,11... | collective-permute-start | bytes 393224 | tf_op jit(solution)/shard_map/ppermute | solution.py:86
  8.8 7.7 %collective-permute-start.1 = (bf16[2,128,256]{2,1,0:T(8,128)(2,1)S(1)}, bf16[2,128,256]{2,1,0:T(8,128)(2,1)S(1)}, u32[]{:S(2)}, u32[]{:S(2)}) collective-permute-start(bf16[2,128,256]{2,1,0:T(8,128)(2,1)S(1)} %pad_maximum_fusion.1), channel_id=1, source_target_pairs={{0,8},{4,12},{8,0},{12,4},{16,24},{20,28},{24,16},{28,20},{1,9},{5... | collective-permute-start | bytes 393224 | tf_op jit(solution)/shard_map/ppermute | solution.py:86
  13.6 5.0 %collective-permute-start.5 = (bf16[1,2,128,256]{3,2,1,0:T(8,128)(2,1)S(1)}, bf16[1,2,128,256]{3,2,1,0:T(8,128)(2,1)S(1)}, u32[]{:S(2)}, u32[]{:S(2)}) collective-permute-start(bf16[1,2,128,256]{3,2,1,0:T(8,128)(2,1)S(1)} %collective-permute-done.4.refs_7_), channel_id=1, source_target_pairs={{0,1},{1,0},{2,3},{3,2},{4,5},{5,4},{6,7},{7,6},{8,9},{9,8},{10,11... | collective-permute-start | bytes 393224 | tf_op jit(solution)/shard_map/ppermute | solution.py:86
  15.0 10.4 %collective-permute-start.11 = (bf16[1,128,256]{2,1,0:T(8,128)(2,1)S(1)}, bf16[1,128,256]{2,1,0:T(8,128)(2,1)S(1)}, u32[]{:S(2)}, u32[]{:S(2)}) collective-permute-start(bf16[1,128,256]{2,1,0:T(8,128)(2,1)S(1)} %get-tuple-element.27.refs_10_), channel_id=1, source_target_pairs={{0,8},{4,12},{8,0},{12,4},{16,24},{20,28},{24,16},{28,20},{1,9},{5... | collective-permute-start | bytes 196616 | tf_op jit(solution)/shard_map/ppermute | solution.py:86
  16.5 2.1 %collective-permute-start.2 = (bf16[1,4,128,256]{3,2,1,0:T(8,128)(2,1)S(1)}, bf16[1,4,128,256]{3,2,1,0:T(8,128)(2,1)S(1)}, u32[]{:S(2)}, u32[]{:S(2)}) collective-permute-start(bf16[1,4,128,256]{3,2,1,0:T(8,128)(2,1)S(1)} %maximum_bitcast_fusion), channel_id=1, source_target_pairs={{0,4},{4,0},{8,12},{12,8},{16,20},{20,16},{24,28},{28,24},{1,5},{5... | collective-permute-start | bytes 786440 | tf_op jit(solution)/shard_map/ppermute | solution.py:264
  19.0 9.1 %collective-permute-start.7 = (bf16[1,2,128,256]{3,2,1,0:T(8,128)(2,1)S(1)}, bf16[1,2,128,256]{3,2,1,0:T(8,128)(2,1)S(1)}, u32[]{:S(2)}, u32[]{:S(2)}) collective-permute-start(bf16[1,2,128,256]{3,2,1,0:T(8,128)(2,1)S(1)} %bitcast.30), channel_id=1, source_target_pairs={{0,2},{1,3},{2,0},{3,1},{4,6},{5,7},{6,4},{7,5},{8,10},{9,11},{10,... | collective-permute-start | bytes 393224 | tf_op jit(solution)/shard_map/ppermute | solution.py:86
  21.5 6.9 %collective-permute-start.6 = (bf16[1,2,128,256]{3,2,1,0:T(8,128)(2,1)S(1)}, bf16[1,2,128,256]{3,2,1,0:T(8,128)(2,1)S(1)}, u32[]{:S(2)}, u32[]{:S(2)}) collective-permute-start(bf16[1,2,128,256]{3,2,1,0:T(8,128)(2,1)S(1)} %bitcast.31), channel_id=1, source_target_pairs={{0,1},{1,0},{2,3},{3,2},{4,5},{5,4},{6,7},{7,6},{8,9},{9,8},{10,11... | collective-permute-start | bytes 393224 | tf_op jit(solution)/shard_map/ppermute | solution.py:86
  23.3 4.3 %collective-permute-start.9 = (bf16[1,128,256]{2,1,0:T(8,128)(2,1)S(1)}, bf16[1,128,256]{2,1,0:T(8,128)(2,1)S(1)}, u32[]{:S(2)}, u32[]{:S(2)}) collective-permute-start(bf16[1,128,256]{2,1,0:T(8,128)(2,1)S(1)} %get-tuple-element.36.refs_5_), channel_id=1, source_target_pairs={{0,8},{4,12},{8,0},{12,4},{16,24},{20,28},{24,16},{28,20},{1,9},{5... | collective-permute-start | bytes 196616 | tf_op jit(solution)/shard_map/ppermute | solution.py:86
  24.8 6.0 %collective-permute-start.10 = (bf16[1,2,128,256]{3,2,1,0:T(8,128)(2,1)S(1)}, bf16[1,2,128,256]{3,2,1,0:T(8,128)(2,1)S(1)}, u32[]{:S(2)}, u32[]{:S(2)}) collective-permute-start(bf16[1,2,128,256]{3,2,1,0:T(8,128)(2,1)S(1)} %pad_maximum_fusion.2), channel_id=1, source_target_pairs={{0,16},{4,20},{8,24},{12,28},{16,0},{20,4},{24,8},{28,12},{1,17},{... | collective-permute-start | bytes 393224 | tf_op jit(solution)/shard_map/ppermute | solution.py:86
  27.6 5.0 %collective-permute-start.12 = (bf16[1,2,128,256]{3,2,1,0:T(8,128)(2,1)S(1)}, bf16[1,2,128,256]{3,2,1,0:T(8,128)(2,1)S(1)}, u32[]{:S(2)}, u32[]{:S(2)}) collective-permute-start(bf16[1,2,128,256]{3,2,1,0:T(8,128)(2,1)S(1)} %pad_maximum_fusion.3), channel_id=1, source_target_pairs={{0,16},{4,20},{8,24},{12,28},{16,0},{20,4},{24,8},{28,12},{1,17},{... | collective-permute-start | bytes 393224 | tf_op jit(solution)/shard_map/ppermute | solution.py:86
  28.4 5.0 %collective-permute-start.8 = (bf16[1,2,128,256]{3,2,1,0:T(8,128)(2,1)S(1)}, bf16[1,2,128,256]{3,2,1,0:T(8,128)(2,1)S(1)}, u32[]{:S(2)}, u32[]{:S(2)}) collective-permute-start(bf16[1,2,128,256]{3,2,1,0:T(8,128)(2,1)S(1)} %collective-permute-done.7.refs_4_), channel_id=1, source_target_pairs={{0,1},{1,0},{2,3},{3,2},{4,5},{5,4},{6,7},{7,6},{8,9},{9,8},{10,11... | collective-permute-start | bytes 393224 | tf_op jit(solution)/shard_map/ppermute | solution.py:86
  32.8 2.0 %collective-permute-start.13 = (bf16[2,4,128,256]{3,2,1,0:T(8,128)(2,1)S(1)}, bf16[2,4,128,256]{3,2,1,0:T(8,128)(2,1)S(1)}, u32[]{:S(2)}, u32[]{:S(2)}) collective-permute-start(bf16[2,4,128,256]{3,2,1,0:T(8,128)(2,1)S(1)} %pad_maximum_fusion), channel_id=1, source_target_pairs={{0,4},{4,0},{8,12},{12,8},{16,20},{20,16},{24,28},{28,24},{1,5},{5... | collective-permute-start | bytes 1572872 | tf_op jit(solution)/shard_map/ppermute | solution.py:264

commit v5 on v2

--- a/solution.py
+++ b/solution.py
@@ -36,7 +36,7 @@
                 rows = pl.ds(i * block_size, block_size)
                 kept = jnp.zeros((block_size, width), jnp.float32)
                 for j in range(width // block_size):
-                    kept = jnp.where(lane == j, pattern_held[k, i, j].astype(jnp.float32), kept)
+                    kept = jnp.where(lane == j, pattern_held[k, i:i + 1, j:j + 1].astype(jnp.float32), kept)
                 kept_ref[k, rows, :] = kept
                 pair_ref[k, rows, :] = (dense_held[k, rows, :].astype(jnp.float32) * kept).astype(pair_ref.dtype)
 
@@ -50,7 +50,7 @@
         in_specs=[IN_HBM] * 4,
         out_specs=(IN_VMEM, IN_VMEM),
         scratch_shapes=[
-            pltpu.SMEM((2,) + block_pattern.shape, jnp.int32),
+            pltpu.VMEM((2,) + block_pattern.shape, jnp.int32),
             pltpu.VMEM((2, height, width), density.dtype),
             pltpu.SemaphoreType.DMA((4,)),
         ],

time: 34.9 us -> 35 us (level)
  no operation moved by 1% of the time
where the time goes in v5:
time: 35 us; the launch traced here: 34.8 us
  starting transfers between devices  20.9 us (60%)
  waiting for transfers between devices  10.1 us (29%)
  Pallas kernels  2.87 us (8%)
  between operations  0.75 us (2%)
    ppermute x13, starting transfers between devices, swap(): lax.ppermute(blocks, axis_name, [(i, i ^ flip) for i in range(size)])  20.7 us
    ppermute x13, waiting for transfers between devices, swap(): lax.ppermute(blocks, axis_name, [(i, i ^ flip) for i in range(size)])  10.1 us
    pallas_call x3, Pallas kernels, call(): pl.pallas_call(body, out_shape=out_shape, in_specs=[IN_VMEM] * len(arrays...  1.79 us
    pallas_call x1, Pallas kernels, mask(): pl.pallas_call(kernel, out_shape=(pltpu.VMEM((2, height, width), density....  1.07 us
  transfers between devices with their start and end apart: 15, of which 8 were waited for; matrix products, arithmetic and copies ran while one was open for 1% of the time, Pallas kernels for 2%

profile of v5, /device:TPU:0, one launch (start us, length us, event | category | flops | bytes accessed | tf_op | source)
XLA Modules:
  0.0 34.8 jit_solution(5699874971165223646)
XLA Ops:
  0.6 1.1 %mask.1 = (bf16[2,128,256]{2,1,0:T(8,128)(2,1)S(1)}, f32[2,128,256]{2,1,0:T(8,128)S(1)}) custom-call(s32[2,4]{1,0:T(2,128)} %refs_0_.1, s32[2,4]{1,0:T(2,128)} %refs_1_.1, bf16[128,256]{1,0:T(8,128)(2,1)} %refs_2_.1, bf16[128,256]{1,0:T(8,128)(2,1)} %refs_3_.1), custom_call_target="tpu_custom_call" | custom-call | tf_op jit(solution)/shard_map/mask/pallas_call | solution.py:44
  1.7 4.1 %collective-permute-start.5 = (bf16[1,2,128,256]{3,2,1,0:T(8,128)(2,1)S(1)}, bf16[1,2,128,256]{3,2,1,0:T(8,128)(2,1)S(1)}, u32[]{:S(2)}, u32[]{:S(2)}) collective-permute-start(bf16[1,2,128,256]{3,2,1,0:T(8,128)(2,1)S(1)} %bitcast.24), channel_id=1, source_target_pairs={{0,2},{1,3},{2,0},{3,1},{4,6},{5,7},{6,4},{7,5},{8,10},{9,11},{10,... | collective-permute-start | bytes 393224 | tf_op jit(solution)/shard_map/ppermute | solution.py:86
  5.8 1.6 %collective-permute-start.4 = (bf16[1,2,128,256]{3,2,1,0:T(8,128)(2,1)S(1)}, bf16[1,2,128,256]{3,2,1,0:T(8,128)(2,1)S(1)}, u32[]{:S(2)}, u32[]{:S(2)}) collective-permute-start(bf16[1,2,128,256]{3,2,1,0:T(8,128)(2,1)S(1)} %bitcast.25), channel_id=1, source_target_pairs={{0,1},{1,0},{2,3},{3,2},{4,5},{5,4},{6,7},{7,6},{8,9},{9,8},{10,11... | collective-permute-start | bytes 393224 | tf_op jit(solution)/shard_map/ppermute | solution.py:86
  7.4 1.6 %collective-permute-start = (bf16[1,128,256]{2,1,0:T(8,128)(2,1)S(1)}, bf16[1,128,256]{2,1,0:T(8,128)(2,1)S(1)}, u32[]{:S(2)}, u32[]{:S(2)}) collective-permute-start(bf16[1,128,256]{2,1,0:T(8,128)(2,1)S(1)} %get-tuple-element.34.refs_2_), channel_id=1, source_target_pairs={{0,16},{4,20},{8,24},{12,28},{16,0},{20,4},{24,8},{28,12},{1,17},{... | collective-permute-start | bytes 196616 | tf_op jit(solution)/shard_map/ppermute | solution.py:86
  9.0 1.5 %collective-permute-start.1 = (bf16[1,128,256]{2,1,0:T(8,128)(2,1)S(1)}, bf16[1,128,256]{2,1,0:T(8,128)(2,1)S(1)}, u32[]{:S(2)}, u32[]{:S(2)}) collective-permute-start(bf16[1,128,256]{2,1,0:T(8,128)(2,1)S(1)} %get-tuple-element.34.refs_2_), channel_id=1, source_target_pairs={{0,8},{4,12},{8,0},{12,4},{16,24},{20,28},{24,16},{28,20},{1,9},{5... | collective-permute-start | bytes 196616 | tf_op jit(solution)/shard_map/ppermute | solution.py:86
  10.5 1.3 %collective-permute-done.refs_3_ = bf16[1,128,256]{2,1,0:T(8,128)(2,1)S(1)} collective-permute-done((bf16[1,128,256]{2,1,0:T(8,128)(2,1)S(1)}, bf16[1,128,256]{2,1,0:T(8,128)(2,1)S(1)}, u32[]{:S(2)}, u32[]{:S(2)}) %collective-permute-start) | collective-permute-done | bytes 65568 | tf_op jit(solution)/shard_map/ppermute | solution.py:86
  11.7 1.5 %collective-permute-start.2 = (bf16[1,128,256]{2,1,0:T(8,128)(2,1)S(1)}, bf16[1,128,256]{2,1,0:T(8,128)(2,1)S(1)}, u32[]{:S(2)}, u32[]{:S(2)}) collective-permute-start(bf16[1,128,256]{2,1,0:T(8,128)(2,1)S(1)} %collective-permute-done.refs_3_), channel_id=1, source_target_pairs={{0,8},{4,12},{8,0},{12,4},{16,24},{20,28},{24,16},{28,20},{1,9},{5... | collective-permute-start | bytes 196616 | tf_op jit(solution)/shard_map/ppermute | solution.py:86
  13.2 0.6 %collective-permute-start.6 = (bf16[1,2,128,256]{3,2,1,0:T(8,128)(2,1)S(1)}, bf16[1,2,128,256]{3,2,1,0:T(8,128)(2,1)S(1)}, u32[]{:S(2)}, u32[]{:S(2)}) collective-permute-start(bf16[1,2,128,256]{3,2,1,0:T(8,128)(2,1)S(1)} %collective-permute-done.5.refs_8_), channel_id=1, source_target_pairs={{0,1},{1,0},{2,3},{3,2},{4,5},{5,4},{6,7},{7,6},{8,9},{9,8},{10,11... | collective-permute-start | bytes 393224 | tf_op jit(solution)/shard_map/ppermute | solution.py:86
  13.9 1.5 %collective-permute-start.12 = (bf16[1,128,256]{2,1,0:T(8,128)(2,1)S(1)}, bf16[1,128,256]{2,1,0:T(8,128)(2,1)S(1)}, u32[]{:S(2)}, u32[]{:S(2)}) collective-permute-start(bf16[1,128,256]{2,1,0:T(8,128)(2,1)S(1)} %get-tuple-element.27.refs_10_), channel_id=1, source_target_pairs={{0,8},{4,12},{8,0},{12,4},{16,24},{20,28},{24,16},{28,20},{1,9},{5... | collective-permute-start | bytes 196616 | tf_op jit(solution)/shard_map/ppermute | solution.py:86
  15.4 1.2 %collective-permute-done.2.refs_5_ = bf16[1,128,256]{2,1,0:T(8,128)(2,1)S(1)} collective-permute-done((bf16[1,128,256]{2,1,0:T(8,128)(2,1)S(1)}, bf16[1,128,256]{2,1,0:T(8,128)(2,1)S(1)}, u32[]{:S(2)}, u32[]{:S(2)}) %collective-permute-start.2) | collective-permute-done | bytes 65568 | tf_op jit(solution)/shard_map/ppermute | solution.py:86
  16.7 1.5 %collective-permute-done.6.block_ref = bf16[1,2,128,256]{3,2,1,0:T(8,128)(2,1)S(1)} collective-permute-done((bf16[1,2,128,256]{3,2,1,0:T(8,128)(2,1)S(1)}, bf16[1,2,128,256]{3,2,1,0:T(8,128)(2,1)S(1)}, u32[]{:S(2)}, u32[]{:S(2)}) %collective-permute-start.6) | collective-permute-done | bytes 131104 | tf_op jit(solution)/shard_map/ppermute | solution.py:86
  18.2 0.4 %square_step.1 = (bf16[2,128,256]{2,1,0:T(8,128)(2,1)S(1)}, bf16[1024,256]{1,0:T(8,128)(2,1)S(1)}, bf16[256,1024]{1,0:T(8,128)(2,1)S(1)}) custom-call(bf16[2,128,256]{2,1,0:T(8,128)(2,1)S(1)} %get-tuple-element.16.refs_0_, f32[2,128,256]{2,1,0:T(8,128)S(1)} %get-tuple-element.15.refs_1_.refs_0_, bf16[1,128,256]{2,1,0:T(8,128)(2,1)S(1)} %get-tuple-element.34.refs_2_, ...), custom_call_target="tpu_custom_call" | custom-call | tf_op jit(solution)/shard_map/square_step/pallas_call | solution.py:161
  18.6 1.8 %collective-permute-start.8 = (bf16[1,2,128,256]{3,2,1,0:T(8,128)(2,1)S(1)}, bf16[1,2,128,256]{3,2,1,0:T(8,128)(2,1)S(1)}, u32[]{:S(2)}, u32[]{:S(2)}) collective-permute-start(bf16[1,2,128,256]{3,2,1,0:T(8,128)(2,1)S(1)} %bitcast.30), channel_id=1, source_target_pairs={{0,2},{1,3},{2,0},{3,1},{4,6},{5,7},{6,4},{7,5},{8,10},{9,11},{10,... | collective-permute-start | bytes 393224 | tf_op jit(solution)/shard_map/ppermute | solution.py:86
  20.4 1.7 %collective-permute-start.7 = (bf16[1,2,128,256]{3,2,1,0:T(8,128)(2,1)S(1)}, bf16[1,2,128,256]{3,2,1,0:T(8,128)(2,1)S(1)}, u32[]{:S(2)}, u32[]{:S(2)}) collective-permute-start(bf16[1,2,128,256]{3,2,1,0:T(8,128)(2,1)S(1)} %bitcast.31), channel_id=1, source_target_pairs={{0,1},{1,0},{2,3},{3,2},{4,5},{5,4},{6,7},{7,6},{8,9},{9,8},{10,11... | collective-permute-start | bytes 393224 | tf_op jit(solution)/shard_map/ppermute | solution.py:86
  22.1 1.5 %collective-permute-start.10 = (bf16[1,128,256]{2,1,0:T(8,128)(2,1)S(1)}, bf16[1,128,256]{2,1,0:T(8,128)(2,1)S(1)}, u32[]{:S(2)}, u32[]{:S(2)}) collective-permute-start(bf16[1,128,256]{2,1,0:T(8,128)(2,1)S(1)} %get-tuple-element.36.refs_5_), channel_id=1, source_target_pairs={{0,8},{4,12},{8,0},{12,4},{16,24},{20,28},{24,16},{28,20},{1,9},{5... | collective-permute-start | bytes 196616 | tf_op jit(solution)/shard_map/ppermute | solution.py:86
  23.7 1.6 %collective-permute-start.11 = (bf16[1,2,128,256]{3,2,1,0:T(8,128)(2,1)S(1)}, bf16[1,2,128,256]{3,2,1,0:T(8,128)(2,1)S(1)}, u32[]{:S(2)}, u32[]{:S(2)}) collective-permute-start(bf16[1,2,128,256]{3,2,1,0:T(8,128)(2,1)S(1)} %pad_maximum_fusion.1), channel_id=1, source_target_pairs={{0,16},{4,20},{8,24},{12,28},{16,0},{20,4},{24,8},{28,12},{1,17},{... | collective-permute-start | bytes 393224 | tf_op jit(solution)/shard_map/ppermute | solution.py:86
  25.2 1.2 %collective-permute-done.10.refs_6_ = bf16[1,128,256]{2,1,0:T(8,128)(2,1)S(1)} collective-permute-done((bf16[1,128,256]{2,1,0:T(8,128)(2,1)S(1)}, bf16[1,128,256]{2,1,0:T(8,128)(2,1)S(1)}, u32[]{:S(2)}, u32[]{:S(2)}) %collective-permute-start.10) | collective-permute-done | bytes 65568 | tf_op jit(solution)/shard_map/ppermute | solution.py:86
  26.4 1.6 %collective-permute-start.13 = (bf16[1,2,128,256]{3,2,1,0:T(8,128)(2,1)S(1)}, bf16[1,2,128,256]{3,2,1,0:T(8,128)(2,1)S(1)}, u32[]{:S(2)}, u32[]{:S(2)}) collective-permute-start(bf16[1,2,128,256]{3,2,1,0:T(8,128)(2,1)S(1)} %pad_maximum_fusion.2), channel_id=1, source_target_pairs={{0,16},{4,20},{8,24},{12,28},{16,0},{20,4},{24,8},{28,12},{1,17},{... | collective-permute-start | bytes 393224 | tf_op jit(solution)/shard_map/ppermute | solution.py:86
  28.1 0.2 collective-permute-start.9
  28.3 1.3 %collective-permute-done.11 = bf16[1,2,128,256]{3,2,1,0:T(8,128)(2,1)S(1)} collective-permute-done((bf16[1,2,128,256]{3,2,1,0:T(8,128)(2,1)S(1)}, bf16[1,2,128,256]{3,2,1,0:T(8,128)(2,1)S(1)}, u32[]{:S(2)}, u32[]{:S(2)}) %collective-permute-start.11) | collective-permute-done | bytes 131104 | tf_op jit(solution)/shard_map/ppermute | solution.py:86
  29.7 1.8 %collective-permute-done.13 = bf16[1,2,128,256]{3,2,1,0:T(8,128)(2,1)S(1)} collective-permute-done((bf16[1,2,128,256]{3,2,1,0:T(8,128)(2,1)S(1)}, bf16[1,2,128,256]{3,2,1,0:T(8,128)(2,1)S(1)}, u32[]{:S(2)}, u32[]{:S(2)}) %collective-permute-start.13) | collective-permute-done | bytes 131104 | tf_op jit(solution)/shard_map/ppermute | solution.py:86
  31.7 1.7 %collective-permute-done.9.refs_6_ = bf16[1,2,128,256]{3,2,1,0:T(8,128)(2,1)S(1)} collective-permute-done((bf16[1,2,128,256]{3,2,1,0:T(8,128)(2,1)S(1)}, bf16[1,2,128,256]{3,2,1,0:T(8,128)(2,1)S(1)}, u32[]{:S(2)}, u32[]{:S(2)}) %collective-permute-start.9) | collective-permute-done | bytes 131104 | tf_op jit(solution)/shard_map/ppermute | solution.py:86
  33.4 0.4 %purify_step.1 = (bf16[128,256]{1,0:T(8,128)(2,1)S(1)}, f32[128,256]{1,0:T(8,128)S(1)}, bf16[128,1024]{1,0:T(8,128)(2,1)S(1)}) custom-call(bf16[2,128,256]{2,1,0:T(8,128)(2,1)S(1)} %get-tuple-element.19.refs_0_, f32[2,128,256]{2,1,0:T(8,128)S(1)} %get-tuple-element.15.refs_1_.refs_0_, bf16[1024,256]{1,0:T(8,128)(2,1)S(1)} %get-tuple-element.20.refs_2_, ...), custom_call_target="tpu_custom_call" | custom-call | flops 6000000000 | tf_op jit(solution)/shard_map/purify_step/pallas_call | solution.py:161
  33.8 1.0 %last_step.1 = (bf16[128,256]{1,0:T(8,128)(2,1)}, bf16[128,256]{1,0:T(8,128)(2,1)}) custom-call(f32[2,128,256]{2,1,0:T(8,128)S(1)} %get-tuple-element.15.refs_1_.refs_0_, bf16[128,256]{1,0:T(8,128)(2,1)S(1)} %get-tuple-element.23.refs_1_, f32[128,256]{1,0:T(8,128)S(1)} %get-tuple-element.24.refs_2_, bf16[256,1024]{1,0:T(8,128)(2,1)S(1)} %get-tuple-element.25.refs_3_, ...), custom_call_target="tpu_custom_call" | custom-call | tf_op jit(solution)/shard_map/last_step/pallas_call | solution.py:161
  (20 shorter events, 0.5 us)
Async XLA Ops:
  1.7 11.5 %collective-permute-start.5 = (bf16[1,2,128,256]{3,2,1,0:T(8,128)(2,1)S(1)}, bf16[1,2,128,256]{3,2,1,0:T(8,128)(2,1)S(1)}, u32[]{:S(2)}, u32[]{:S(2)}) collective-permute-start(bf16[1,2,128,256]{3,2,1,0:T(8,128)(2,1)S(1)} %bitcast.24), channel_id=1, source_target_pairs={{0,2},{1,3},{2,0},{3,1},{4,6},{5,7},{6,4},{7,5},{8,10},{9,11},{10,... | collective-permute-start | bytes 393224 | tf_op jit(solution)/shard_map/ppermute | solution.py:86
  5.8 7.4 %collective-permute-start.4 = (bf16[1,2,128,256]{3,2,1,0:T(8,128)(2,1)S(1)}, bf16[1,2,128,256]{3,2,1,0:T(8,128)(2,1)S(1)}, u32[]{:S(2)}, u32[]{:S(2)}) collective-permute-start(bf16[1,2,128,256]{3,2,1,0:T(8,128)(2,1)S(1)} %bitcast.25), channel_id=1, source_target_pairs={{0,1},{1,0},{2,3},{3,2},{4,5},{5,4},{6,7},{7,6},{8,9},{9,8},{10,11... | collective-permute-start | bytes 393224 | tf_op jit(solution)/shard_map/ppermute | solution.py:86
  7.4 4.3 %collective-permute-start = (bf16[1,128,256]{2,1,0:T(8,128)(2,1)S(1)}, bf16[1,128,256]{2,1,0:T(8,128)(2,1)S(1)}, u32[]{:S(2)}, u32[]{:S(2)}) collective-permute-start(bf16[1,128,256]{2,1,0:T(8,128)(2,1)S(1)} %get-tuple-element.34.refs_2_), channel_id=1, source_target_pairs={{0,16},{4,20},{8,24},{12,28},{16,0},{20,4},{24,8},{28,12},{1,17},{... | collective-permute-start | bytes 196616 | tf_op jit(solution)/shard_map/ppermute | solution.py:86
  9.0 6.4 %collective-permute-start.1 = (bf16[1,128,256]{2,1,0:T(8,128)(2,1)S(1)}, bf16[1,128,256]{2,1,0:T(8,128)(2,1)S(1)}, u32[]{:S(2)}, u32[]{:S(2)}) collective-permute-start(bf16[1,128,256]{2,1,0:T(8,128)(2,1)S(1)} %get-tuple-element.34.refs_2_), channel_id=1, source_target_pairs={{0,8},{4,12},{8,0},{12,4},{16,24},{20,28},{24,16},{28,20},{1,9},{5... | collective-permute-start | bytes 196616 | tf_op jit(solution)/shard_map/ppermute | solution.py:86
  11.7 4.8 %collective-permute-start.2 = (bf16[1,128,256]{2,1,0:T(8,128)(2,1)S(1)}, bf16[1,128,256]{2,1,0:T(8,128)(2,1)S(1)}, u32[]{:S(2)}, u32[]{:S(2)}) collective-permute-start(bf16[1,128,256]{2,1,0:T(8,128)(2,1)S(1)} %collective-permute-done.refs_3_), channel_id=1, source_target_pairs={{0,8},{4,12},{8,0},{12,4},{16,24},{20,28},{24,16},{28,20},{1,9},{5... | collective-permute-start | bytes 196616 | tf_op jit(solution)/shard_map/ppermute | solution.py:86
  13.2 5.0 %collective-permute-start.6 = (bf16[1,2,128,256]{3,2,1,0:T(8,128)(2,1)S(1)}, bf16[1,2,128,256]{3,2,1,0:T(8,128)(2,1)S(1)}, u32[]{:S(2)}, u32[]{:S(2)}) collective-permute-start(bf16[1,2,128,256]{3,2,1,0:T(8,128)(2,1)S(1)} %collective-permute-done.5.refs_8_), channel_id=1, source_target_pairs={{0,1},{1,0},{2,3},{3,2},{4,5},{5,4},{6,7},{7,6},{8,9},{9,8},{10,11... | collective-permute-start | bytes 393224 | tf_op jit(solution)/shard_map/ppermute | solution.py:86
  13.9 11.4 %collective-permute-start.12 = (bf16[1,128,256]{2,1,0:T(8,128)(2,1)S(1)}, bf16[1,128,256]{2,1,0:T(8,128)(2,1)S(1)}, u32[]{:S(2)}, u32[]{:S(2)}) collective-permute-start(bf16[1,128,256]{2,1,0:T(8,128)(2,1)S(1)} %get-tuple-element.27.refs_10_), channel_id=1, source_target_pairs={{0,8},{4,12},{8,0},{12,4},{16,24},{20,28},{24,16},{28,20},{1,9},{5... | collective-permute-start | bytes 196616 | tf_op jit(solution)/shard_map/ppermute | solution.py:86
  16.6 1.6 %collective-permute-start.3 = (bf16[1,4,128,256]{3,2,1,0:T(8,128)(2,1)S(1)}, bf16[1,4,128,256]{3,2,1,0:T(8,128)(2,1)S(1)}, u32[]{:S(2)}, u32[]{:S(2)}) collective-permute-start(bf16[1,4,128,256]{3,2,1,0:T(8,128)(2,1)S(1)} %maximum_bitcast_fusion), channel_id=1, source_target_pairs={{0,4},{4,0},{8,12},{12,8},{16,20},{20,16},{24,28},{28,24},{1,5},{5... | collective-permute-start | bytes 786440 | tf_op jit(solution)/shard_map/ppermute | solution.py:264
  18.6 9.4 %collective-permute-start.8 = (bf16[1,2,128,256]{3,2,1,0:T(8,128)(2,1)S(1)}, bf16[1,2,128,256]{3,2,1,0:T(8,128)(2,1)S(1)}, u32[]{:S(2)}, u32[]{:S(2)}) collective-permute-start(bf16[1,2,128,256]{3,2,1,0:T(8,128)(2,1)S(1)} %bitcast.30), channel_id=1, source_target_pairs={{0,2},{1,3},{2,0},{3,1},{4,6},{5,7},{6,4},{7,5},{8,10},{9,11},{10,... | collective-permute-start | bytes 393224 | tf_op jit(solution)/shard_map/ppermute | solution.py:86
  20.4 7.7 %collective-permute-start.7 = (bf16[1,2,128,256]{3,2,1,0:T(8,128)(2,1)S(1)}, bf16[1,2,128,256]{3,2,1,0:T(8,128)(2,1)S(1)}, u32[]{:S(2)}, u32[]{:S(2)}) collective-permute-start(bf16[1,2,128,256]{3,2,1,0:T(8,128)(2,1)S(1)} %bitcast.31), channel_id=1, source_target_pairs={{0,1},{1,0},{2,3},{3,2},{4,5},{5,4},{6,7},{7,6},{8,9},{9,8},{10,11... | collective-permute-start | bytes 393224 | tf_op jit(solution)/shard_map/ppermute | solution.py:86
  22.1 4.3 %collective-permute-start.10 = (bf16[1,128,256]{2,1,0:T(8,128)(2,1)S(1)}, bf16[1,128,256]{2,1,0:T(8,128)(2,1)S(1)}, u32[]{:S(2)}, u32[]{:S(2)}) collective-permute-start(bf16[1,128,256]{2,1,0:T(8,128)(2,1)S(1)} %get-tuple-element.36.refs_5_), channel_id=1, source_target_pairs={{0,8},{4,12},{8,0},{12,4},{16,24},{20,28},{24,16},{28,20},{1,9},{5... | collective-permute-start | bytes 196616 | tf_op jit(solution)/shard_map/ppermute | solution.py:86
  23.7 6.0 %collective-permute-start.11 = (bf16[1,2,128,256]{3,2,1,0:T(8,128)(2,1)S(1)}, bf16[1,2,128,256]{3,2,1,0:T(8,128)(2,1)S(1)}, u32[]{:S(2)}, u32[]{:S(2)}) collective-permute-start(bf16[1,2,128,256]{3,2,1,0:T(8,128)(2,1)S(1)} %pad_maximum_fusion.1), channel_id=1, source_target_pairs={{0,16},{4,20},{8,24},{12,28},{16,0},{20,4},{24,8},{28,12},{1,17},{... | collective-permute-start | bytes 393224 | tf_op jit(solution)/shard_map/ppermute | solution.py:86
  26.4 5.0 %collective-permute-start.13 = (bf16[1,2,128,256]{3,2,1,0:T(8,128)(2,1)S(1)}, bf16[1,2,128,256]{3,2,1,0:T(8,128)(2,1)S(1)}, u32[]{:S(2)}, u32[]{:S(2)}) collective-permute-start(bf16[1,2,128,256]{3,2,1,0:T(8,128)(2,1)S(1)} %pad_maximum_fusion.2), channel_id=1, source_target_pairs={{0,16},{4,20},{8,24},{12,28},{16,0},{20,4},{24,8},{28,12},{1,17},{... | collective-permute-start | bytes 393224 | tf_op jit(solution)/shard_map/ppermute | solution.py:86
  28.1 5.3 %collective-permute-start.9 = (bf16[1,2,128,256]{3,2,1,0:T(8,128)(2,1)S(1)}, bf16[1,2,128,256]{3,2,1,0:T(8,128)(2,1)S(1)}, u32[]{:S(2)}, u32[]{:S(2)}) collective-permute-start(bf16[1,2,128,256]{3,2,1,0:T(8,128)(2,1)S(1)} %collective-permute-done.8.refs_4_), channel_id=1, source_target_pairs={{0,1},{1,0},{2,3},{3,2},{4,5},{5,4},{6,7},{7,6},{8,9},{9,8},{10,11... | collective-permute-start | bytes 393224 | tf_op jit(solution)/shard_map/ppermute | solution.py:86
  31.6 2.2 %collective-permute-start.14 = (bf16[2,4,128,256]{3,2,1,0:T(8,128)(2,1)S(1)}, bf16[2,4,128,256]{3,2,1,0:T(8,128)(2,1)S(1)}, u32[]{:S(2)}, u32[]{:S(2)}) collective-permute-start(bf16[2,4,128,256]{3,2,1,0:T(8,128)(2,1)S(1)} %pad_maximum_fusion), channel_id=1, source_target_pairs={{0,4},{4,0},{8,12},{12,8},{16,20},{20,16},{24,28},{28,24},{1,5},{5... | collective-permute-start | bytes 1572872 | tf_op jit(solution)/shard_map/ppermute | solution.py:264
